TPU v7x, 32 devices: a whole 2x2x4 slice. The times are simulated.
32 devices in a mesh: rows: 16 (over z, y, core), pairs: 2 (over x).
Axes of the slice: x: 2, y: 2, z: 4, core: 2. Of those that a mesh axis runs over, the one named last changes fastest.
Arguments:
- loads: float32 [4096, 4096], P('rows', 'pairs'), may hold values from -6 to 6
- col_weights: float32 [4096], P('pairs'), may hold values from 0.3 to 3
- partner_offsets: int32 [2, 2], replicated, may hold values from 0 to 127
- skip_mask: int32 [2, 16], P(None, 'pairs'), may hold values 0 or 1
Outputs:
- rotated: float32 [4096, 4096], P('rows', 'pairs')
- column_power: float32 [4096], P('pairs')
All inputs are finite; a program needn't handle non-finite values. No bound on the sum of `skip_mask` on one device may be relied on, other than what follows from the above.
Results may differ from a plain program's by a relative error of at most 0.0003.
Values sent between devices are 32-bit elements; how exact they have to be, the bound alone decides.
A program may use at most 128 MiB of HBM per device.

v0:
```python
import jax
import jax.numpy as jnp
from jax import lax
from jax.sharding import PartitionSpec as P

BLOCK = 128
STEPS = 2


precise = lax.Precision.HIGHEST


def shifted(x, axis, by):
    size = lax.axis_size(axis)
    pairs = [(i, i + by) for i in range(size) if 0 <= i + by < size]
    return lax.ppermute(x, axis, pairs)


def turn_columns(matrix, cosine_values, sine_values, offset):
    half_width = matrix.shape[-1] // 2
    left_part = matrix[..., :half_width]
    right_part = jnp.roll(matrix[..., half_width:], -offset, axis=-1)
    cosine_grid = cosine_values[:, None, :]
    sine_grid = sine_values[:, None, :]
    new_left = cosine_grid * left_part - sine_grid * right_part
    new_right = jnp.roll(sine_grid * left_part + cosine_grid * right_part, offset, axis=-1)
    return jnp.concatenate([new_left, new_right], axis=-1)


def rotate_pair(gram_matrix, offsets_step, skip_step):
    half_width = gram_matrix.shape[-1] // 2
    identity = jnp.broadcast_to(jnp.eye(2 * half_width, dtype=jnp.float32), gram_matrix.shape)
    turned = gram_matrix
    rotation = identity
    for step_round in range(offsets_step.shape[0]):
        offset = offsets_step[step_round]
        diagonal_values = jnp.diagonal(turned, axis1=1, axis2=2)
        first_norms = diagonal_values[:, :half_width]
        second_norms = jnp.roll(diagonal_values[:, half_width:], -offset, axis=1)
        coupling = jnp.diagonal(
            jnp.roll(turned[:, :half_width, half_width:], -offset, axis=2), axis1=1, axis2=2
        )
        half_gap = 0.5 * (second_norms - first_norms)
        gap_sign = jnp.where(half_gap >= 0.0, 1.0, -1.0)
        denominator = jnp.maximum(
            jnp.abs(half_gap) + jnp.sqrt(half_gap * half_gap + coupling * coupling),
            1e-06 * (first_norms + second_norms),
        )
        tangent = gap_sign * coupling / denominator
        cosine_values = 1.0 / jnp.sqrt(1.0 + tangent * tangent)
        sine_values = tangent * cosine_values
        turned = turn_columns(turned, cosine_values, sine_values, offset)
        turned = jnp.swapaxes(
            turn_columns(jnp.swapaxes(turned, 1, 2), cosine_values, sine_values, offset), 1, 2
        )
        rotation = turn_columns(rotation, cosine_values, sine_values, offset)
    unskipped = (skip_step == 0)[:, None, None]
    return (jnp.where(unskipped, rotation, identity), jnp.where(unskipped, turned, gram_matrix))


def whole_gram(joined):
    partial_gram = jnp.einsum(
        "prc,prd->pcd", joined, joined, precision=precise, preferred_element_type=jnp.float32
    )
    return lax.psum(partial_gram, "rows")


def next_gram(joined):
    gram_matrix = whole_gram(joined)
    return gram_matrix


def settle(upper_stack, lower_stack, incoming_upper, incoming_lower, position, last_index):
    head_upper = jnp.concatenate([upper_stack[:1], lower_stack[:1], upper_stack[1:-1]], axis=0)
    rest_upper = jnp.concatenate([incoming_upper[None], upper_stack[:-1]], axis=0)
    new_upper = jnp.where(position == 0, head_upper, rest_upper)
    tail_lower = jnp.concatenate([lower_stack[1:], upper_stack[-1:]], axis=0)
    rest_lower = jnp.concatenate([lower_stack[1:], incoming_lower[None]], axis=0)
    new_lower = jnp.where(position == last_index, tail_lower, rest_lower)
    return (new_upper, new_lower)


def move_all(upper_blocks, lower_blocks, diag_upper, diag_lower, position, last_index):
    incoming_upper = shifted(upper_blocks[-1], "pairs", 1)
    incoming_lower = shifted(lower_blocks[0], "pairs", -1)
    upper_blocks, lower_blocks = settle(
        upper_blocks, lower_blocks, incoming_upper, incoming_lower, position, last_index
    )
    return (upper_blocks, lower_blocks, diag_upper, diag_lower)


def per_device(loads, col_weights, partner_offsets, skip_mask):
    row_count = loads.shape[0]
    half_count = loads.shape[1] // (2 * BLOCK)
    weighted = loads * col_weights[None, :]
    stacked = weighted.reshape(row_count, 2, half_count, BLOCK).transpose(1, 2, 0, 3)
    upper_blocks = stacked[0]
    lower_blocks = stacked[1]
    position = lax.axis_index("pairs")
    last_index = lax.axis_size("pairs") - 1
    diag_upper = jnp.zeros((half_count, BLOCK, BLOCK), jnp.float32)
    diag_lower = jnp.zeros((half_count, BLOCK, BLOCK), jnp.float32)
    turned = jnp.zeros((half_count, 2 * BLOCK, 2 * BLOCK), jnp.float32)
    for step_index in range(STEPS):
        joined = jnp.concatenate([upper_blocks, lower_blocks], axis=-1)
        if step_index == 0:
            gram_matrix = whole_gram(joined)
        else:
            gram_matrix = next_gram(joined)
        rotation, turned = rotate_pair(
            gram_matrix, partner_offsets[step_index], skip_mask[step_index]
        )
        joined = jnp.einsum(
            "prc,pcd->prd", joined, rotation, precision=precise, preferred_element_type=jnp.float32
        )
        upper_blocks = joined[..., :BLOCK]
        lower_blocks = joined[..., BLOCK:]
        diag_upper = turned[:, :BLOCK, :BLOCK]
        diag_lower = turned[:, BLOCK:, BLOCK:]
        if step_index + 1 < STEPS:
            upper_blocks, lower_blocks, diag_upper, diag_lower = move_all(
                upper_blocks, lower_blocks, diag_upper, diag_lower, position, last_index
            )
    total_rows = row_count * lax.axis_size("rows")
    upper_power, lower_power = lax.psum(
        (
            jnp.sum(upper_blocks * upper_blocks, axis=1),
            jnp.sum(lower_blocks * lower_blocks, axis=1),
        ),
        "rows",
    )
    column_power = jnp.concatenate([upper_power.reshape(-1), lower_power.reshape(-1)]) / total_rows
    rotated = (
        jnp.stack([upper_blocks, lower_blocks])
        .transpose(2, 0, 1, 3)
        .reshape(row_count, 2 * half_count * BLOCK)
    )
    return (rotated, column_power)


def solution(mesh):
    in_specs = (P("rows", "pairs"), P("pairs"), P(), P(None, "pairs"))
    out_specs = (P("rows", "pairs"), P("pairs"))
    return jax.shard_map(
        per_device, mesh=mesh, in_specs=in_specs, out_specs=out_specs, check_vma=False
    )
```

profile of v0, /device:TPU:0, one launch (start us, length us, event | category | flops | bytes accessed | tf_op | source)
XLA Modules:
  0.0 427.2 jit_solution(15785190283189077570)
XLA Ops:
  14.2 4.8 %fusion.7 = f32[8,256,256]{2,1,0:T(8,128)} fusion(f32[8,256,128]{2,1,0:T(8,128)S(1)} %get-tuple-element.51, f32[8,256,128]{2,1,0:T(8,128)S(1)} %get-tuple-element.50), kind=kOutput, calls=%fused_computation.56 | convolution fusion | flops 1611137024 | bytes 4194304 | tf_op jit(solution)/shard_map/prc,prd->pcd/dot_general | solution.py:62
  26.7 93.0 %all-reduce.4.cloned.1.call-done = f32[8,256,256]{2,1,0:T(8,128)} async-done(((f32[8,256,256]{2,1,0:T(8,128)}), f32[8,256,256]{2,1,0:T(8,128)}) %all-reduce.4.cloned.1.call-update) | async-done | bytes 2097168 | tf_op jit(solution)/shard_map/psum | solution.py:65
  121.2 4.6 %copy.137 = f32[8,128,128]{0,2,1:T(8,128)} copy(f32[8,128,128]{2,1,0:T(8,128)S(1)} %fusion.40) | data formatting | bytes 1048576 | tf_op jit(solution)/shard_map/jit(_roll_dynamic)/dynamic_slice | solution.py:41
  127.7 16.7 %copy.135 = f32[8,256,256]{0,2,1:T(8,128)} copy(f32[8,256,256]{2,1,0:T(8,128)S(1)} %copy-done.1) | data formatting | bytes 4194304 | tf_op jit(solution)/shard_map/psum | solution.py:65
  144.4 2.3 gather_fusion
  149.0 2.9 multiply_add_fusion.5
  151.9 2.5 copy.140
  155.4 3.1 fusion.32
  158.5 2.5 copy.143
  163.4 16.7 %copy.144 = f32[8,256,256]{0,2,1:T(8,128)} copy(f32[8,256,256]{2,1,0:T(8,128)S(1)} %maximum_bitcast_fusion.1) | data formatting | bytes 4194304 | tf_op jit(solution)/shard_map/transpose | solution.py:53
  181.0 2.3 gather_fusion.2
  185.0 4.6 %copy.146 = f32[8,128,128]{0,2,1:T(8,128)} copy(f32[8,128,128]{2,1,0:T(8,128)S(1)} %fusion.39) | data formatting | bytes 1048576 | tf_op jit(solution)/shard_map/jit(_roll_dynamic)/dynamic_slice | solution.py:41
  194.7 2.4 fusion
  198.6 4.6 %collective-permute-start = (f32[256,128]{0,1:T(8,128)S(1)}, f32[256,128]{0,1:T(8,128)S(1)}, u32[]{:S(2)}, u32[]{:S(2)}) collective-permute-start(f32[256,128]{0,1:T(8,128)S(1)} %get-tuple-element.41), channel_id=1, source_target_pairs={{0,1},{2,3},{4,5},{6,7},{8,9},{10,11},{12,13},{14,15},{16,17},{18,... | collective-permute-start | bytes 393224 | tf_op jit(solution)/shard_map/ppermute | solution.py:16
  206.8 3.6 fusion.6
  215.3 93.4 %all-reduce.6.cloned.1.call-done = f32[8,256,256]{1,2,0:T(8,128)} async-done(((f32[8,256,256]{1,2,0:T(8,128)}), f32[8,256,256]{1,2,0:T(8,128)}) %all-reduce.6.cloned.1.call-update) | async-done | bytes 2097168 | tf_op jit(solution)/shard_map/psum | solution.py:65
  308.7 17.5 %copy.150 = f32[8,256,256]{0,2,1:T(8,128)} copy(f32[8,256,256]{1,2,0:T(8,128)} %all-reduce.6.cloned.1.call-done) | data formatting | bytes 4194304 | tf_op jit(solution)/shard_map/psum | solution.py:65
  326.2 3.0 gather_fusion.4
  331.7 8.3 %copy.152 = f32[8,128,128]{0,2,1:T(8,128)} copy(f32[8,128,128]{1,2,0:T(8,128)} %fusion.38) | data formatting | bytes 1048576 | tf_op jit(solution)/shard_map/jit(_roll_dynamic)/dynamic_slice | solution.py:41
  340.0 2.4 gather_fusion.5
  353.1 16.7 %copy.155 = f32[8,256,256]{0,2,1:T(8,128)} copy(f32[8,256,256]{2,1,0:T(8,128)S(1)} %maximum_bitcast_fusion.2) | data formatting | bytes 4194304 | tf_op jit(solution)/shard_map/transpose | solution.py:53
  370.7 2.3 gather_fusion.6
  374.7 4.6 %copy.157 = f32[8,128,128]{0,2,1:T(8,128)} copy(f32[8,128,128]{2,1,0:T(8,128)S(1)} %fusion.37) | data formatting | bytes 1048576 | tf_op jit(solution)/shard_map/jit(_roll_dynamic)/dynamic_slice | solution.py:41
  388.8 30.9 %all-reduce = (f32[1024]{0:T(1024)S(1)}, f32[1024]{0:T(1024)S(1)}) all-reduce(f32[1024]{0:T(1024)S(1)} %bitcast.127, f32[1024]{0:T(1024)S(1)} %bitcast.126), channel_id=1, replica_groups=mesh['rows'=16,'pairs'=2] {'rows'}, use_global_device_ids=true, to_apply=%region_5.9 | all-reduce | flops 2048 | bytes 16384 | tf_op jit(solution)/shard_map/psum | solution.py:125
  (124 shorter events, 56.6 us)
Async XLA Ops:
  7.2 2.0 copy-start.15
  7.2 112.5 %all-reduce.4.cloned.1.call-start = ((), (), s32[]{:S(2)}) async-start(), calls=%async_computation | async-start | bytes 4194304 | tf_op jit(solution)/shard_map/psum | solution.py:65
  12.9 1.0 copy-start.6
  12.9 1.3 copy-start.8
  19.0 6.5 %copy-start.19 = (s32[2,8]{1,0:T(2,128)S(1)}, s32[2,8]{1,0:T(2,128)}, u32[]{:S(2)}) copy-start(s32[2,8]{1,0:T(2,128)} %param.13) | copy-start | bytes 196
  19.0 289.6 %all-reduce.6.cloned.1.call-start = ((), (), s32[]{:S(2)}) async-start(), calls=%async_computation.1 | async-start | bytes 4194304 | tf_op jit(solution)/shard_map/psum | solution.py:65
  121.2 6.5 %copy-start.1 = (f32[8,256,256]{2,1,0:T(8,128)S(1)}, f32[8,256,256]{2,1,0:T(8,128)}, u32[]{:S(2)}) copy-start(f32[8,256,256]{2,1,0:T(8,128)} %all-reduce.4.cloned.1.call-done) | copy-start | bytes 6291460
  161.0 1.2 copy-start.13
  185.0 6.6 %copy-start.12 = (f32[8,256,128]{1,2,0:T(8,128)S(1)}, f32[8,256,128]{1,2,0:T(8,128)}, u32[]{:S(2)}) copy-start(f32[8,256,128]{1,2,0:T(8,128)} %get-tuple-element.55) | copy-start | bytes 3145732
  193.1 1.2 copy-start.7
  193.1 1.5 copy-start.9
  193.2 1.5 copy-start.18
  197.1 6.9 %collective-permute-start.1 = (f32[256,128]{0,1:T(8,128)S(1)}, f32[256,128]{0,1:T(8,128)S(1)}, u32[]{:S(2)}, u32[]{:S(2)}) collective-permute-start(f32[256,128]{0,1:T(8,128)S(1)} %get-tuple-element.42), channel_id=1, source_target_pairs={{1,0},{3,2},{5,4},{7,6},{9,8},{11,10},{13,12},{15,14},{17,16},{19,... | collective-permute-start | bytes 393224 | tf_op jit(solution)/shard_map/ppermute | solution.py:16
  198.6 7.1 %collective-permute-start = (f32[256,128]{0,1:T(8,128)S(1)}, f32[256,128]{0,1:T(8,128)S(1)}, u32[]{:S(2)}, u32[]{:S(2)}) collective-permute-start(f32[256,128]{0,1:T(8,128)S(1)} %get-tuple-element.41), channel_id=1, source_target_pairs={{0,1},{2,3},{4,5},{6,7},{8,9},{10,11},{12,13},{14,15},{16,17},{18,... | collective-permute-start | bytes 393224 | tf_op jit(solution)/shard_map/ppermute | solution.py:16
  204.1 1.8 copy-start.2
  205.9 1.0 copy-start.4
  308.7 22.0 %copy-start = (f32[8,256,256]{1,2,0:T(8,128)S(1)}, f32[8,256,256]{1,2,0:T(8,128)}, u32[]{:S(2)}) copy-start(f32[8,256,256]{1,2,0:T(8,128)} %all-reduce.6.cloned.1.call-done) | copy-start | bytes 6291460
  330.1 9.9 %copy-start.14 = (f32[256,8]{0,1:T(8,128)}, f32[256,8]{0,1:T(8,128)S(1)}, u32[]{:S(2)}) copy-start(f32[256,8]{0,1:T(8,128)S(1)} %copy.151) | copy-start | bytes 24580
  343.3 1.3 slice-start
  350.3 1.2 copy-start.11
  374.7 6.6 %copy-start.10 = (f32[8,256,128]{1,2,0:T(8,128)S(1)}, f32[8,256,128]{1,2,0:T(8,128)}, u32[]{:S(2)}) copy-start(f32[8,256,128]{1,2,0:T(8,128)} %get-tuple-element.63) | copy-start | bytes 3145732
  382.6 1.2 copy-start.3
  382.6 1.5 copy-start.5
  382.6 1.5 copy-start.17
  (1 other events, 0.7 us)
Sparse Core Ops, SparseCore 0:
  19.1 100.5 all-reduce.3
  210.6 98.0 all-reduce.5
where the time goes:
time: 428 us; the launch traced here: 427 us
  waiting for transfers between devices  189 us (44%)
  local copies, waits for them, and re-layouts  137 us (32%)
  blocking collectives  30.9 us (7%)
  other arithmetic  26.2 us (6%)
  between operations  24.6 us (6%)
  matrix products  13.1 us (3%)
  starting transfers between devices  6.11 us (1%)
    psum x2, waiting for transfers between devices, whole_gram(): return lax.psum(partial_gram, 'rows')  186 us
    psum x2, local copies, waits for them, and re-layouts, whole_gram(): return lax.psum(partial_gram, 'rows')  34.2 us
    transpose x2, local copies, waits for them, and re-layouts, rotate_pair(): jnp.swapaxes(turn_columns(jnp.swapaxes(turned, 1, 2), cosine_values, sine...  33.5 us
    psum x1, blocking collectives, per_device(): lax.psum((jnp.sum(upper_blocks * upper_blocks, axis=1), jnp.sum(lower_blo...  30.9 us
    dynamic_slice x4, local copies, waits for them, and re-layouts, rotate_pair(): jnp.roll(turned[:, :half_width, half_width:], -offset, axis=2)  22.3 us
    gather x8, local copies, waits for them, and re-layouts, rotate_pair(): diagonal_values = jnp.diagonal(turned, axis1=1, axis2=2)  11.1 us
    unnamed x43, local copies, waits for them, and re-layouts  10.6 us
    gather x8, local copies, waits for them, and re-layouts, rotate_pair(): jnp.diagonal(jnp.roll(turned[:, :half_width, half_width:], -offset, axis=...  8.76 us
  transfers between devices with their start and end apart: 4, of which 4 were waited for; matrix products, arithmetic and copies ran while one was open for 1% of the time, Pallas kernels for 0%

commit v1 on v0

v1 whole, which is shorter than its diff:
```python
import functools
import jax
import jax.numpy as jnp
from jax import lax
from jax.experimental import pallas as pl
from jax.experimental.pallas import tpu as pltpu
from jax.sharding import PartitionSpec as P

BLOCK = 128
STEPS = 2
TILE = 8
CHUNK = 64
MESH = pl.DeviceIdType.MESH


def rolled(x, shift):
    return pltpu.roll(x, shift, 1)


def fold(x):
    return jnp.sum(x.reshape(x.shape[0] // TILE, TILE, BLOCK), axis=0)


def shifts_of(offsets, step):
    first, second = offsets[step, 0], offsets[step, 1]
    to_first = lax.rem(BLOCK - first, BLOCK)
    to_second = lax.rem(BLOCK - second, BLOCK)
    between = lax.rem(BLOCK + first - second, BLOCK)
    return to_first, to_second, between, second


def products(upper, lower, shifts, rows, weights, partial):
    to_first, to_second, between, _ = shifts

    def body(at, sums):
        spot = pl.ds(pl.multiple_of(at * CHUNK, CHUNK), CHUNK)
        u, l = upper[spot, :], lower[spot, :]
        if weights is not None:
            u, l = u * weights[0], l * weights[1]
            upper[spot, :] = u
            lower[spot, :] = l
        lp, ud, ld = rolled(l, to_first), rolled(u, between), rolled(l, to_second)
        pairs = ((u, u), (lp, lp), (u, lp), (u, ud), (u, ld), (lp, ud), (lp, ld))
        return tuple(total + fold(a * b) for total, (a, b) in zip(sums, pairs))

    zero = jnp.zeros((TILE, BLOCK), jnp.float32)
    sums = lax.fori_loop(0, rows // CHUNK, body, (zero,) * 7)
    for at, total in enumerate(sums):
        partial[pl.ds(at, 1), :] = jnp.sum(total, axis=0, keepdims=True)
    partial[pl.ds(7, 1), :] = jnp.zeros((1, BLOCK), jnp.float32)


def angle(a, b, g):
    half_gap = 0.5 * (b - a)
    sign = jnp.where(half_gap >= 0.0, 1.0, -1.0)
    denominator = jnp.maximum(
        jnp.abs(half_gap) + jnp.sqrt(half_gap * half_gap + g * g), 1e-06 * (a + b)
    )
    t = sign * g / denominator
    c = 1.0 / jnp.sqrt(1.0 + t * t)
    return c, t * c


def norms(a, b, g, c, s):
    cross = 2.0 * c * s * g
    return c * c * a - cross + s * s * b, s * s * a + cross + c * c * b


def turn(total, skip, shifts):
    _, _, between, back = shifts
    row = [jnp.broadcast_to(total[at : at + 1, :], (TILE, BLOCK)) for at in range(7)]
    a, b, g, u_ud, u_ld, l_ud, l_ld = row
    keep = jnp.full((TILE, BLOCK), skip, jnp.int32) == 0
    c, s = angle(a, b, g)
    c, s = jnp.where(keep, c, 1.0), jnp.where(keep, s, 0.0)
    a1, b1 = norms(a, b, g, c, s)
    cd, sd, bd = rolled(c, between), rolled(s, between), rolled(b1, between)
    g1 = c * (sd * u_ud + cd * u_ld) - s * (sd * l_ud + cd * l_ld)
    c2, s2 = angle(a1, bd, g1)
    c2, s2 = jnp.where(keep, c2, 1.0), jnp.where(keep, s2, 0.0)
    a2, b2 = norms(a1, bd, g1, c2, s2)
    place = lax.broadcasted_iota(jnp.int32, (TILE, BLOCK), 0)
    tile = rolled(b2, back)
    for at, value in enumerate((c, s, cd, sd, c2, s2, a2)):
        tile = jnp.where(place == at, value, tile)
    return tile


def rotate(upper, lower, new_upper, new_lower, coefs, shifts, rows):
    to_first, to_second, between, back = shifts
    tile = coefs[...]
    c, s, cd, sd, c2, s2 = (tile[at : at + 1, :] for at in range(6))
    up = (c2 * c, -c2 * s, -s2 * sd, -s2 * cd)
    low = (s2 * c, -s2 * s, c2 * sd, c2 * cd)

    def body(at, carry):
        spot = pl.ds(pl.multiple_of(at * CHUNK, CHUNK), CHUNK)
        u, l = upper[spot, :], lower[spot, :]
        parts = (u, rolled(l, to_first), rolled(u, between), rolled(l, to_second))
        new_upper[spot, :] = sum(f * x for f, x in zip(up, parts))
        new_lower[spot, :] = rolled(sum(f * x for f, x in zip(low, parts)), back)
        return carry

    lax.fori_loop(0, rows // CHUNK, body, 0)


def kernel(
    n, n_pairs, half, rows,
    loads, weights, offsets, skips,
    rotated, power,
    data, moved, partial, arrived, coefs,
    load_sem, store_sem, sum_sem, pair_sem,
):
    me, position = lax.axis_index("rows"), lax.axis_index("pairs")
    copies = n // half
    own, group = me // copies, lax.rem(me, copies)
    not_first = (position + n_pairs - 1) // n_pairs
    is_last = (position + 1) // n_pairs

    def load(block):
        columns = pl.ds(pl.multiple_of(block * BLOCK, BLOCK), BLOCK)
        return pltpu.make_async_copy(loads.at[:, columns], data.at[block], load_sem.at[block])

    def store(block):
        columns = pl.ds(pl.multiple_of(block * BLOCK, BLOCK), BLOCK)
        return pltpu.make_async_copy(data.at[block], rotated.at[:, columns], store_sem.at[block])

    for k in range(half):
        load(k).start()
        load(half + k).start()

    barrier = pltpu.get_barrier_semaphore()

    @pl.loop(1, n)
    def _(by):
        pl.semaphore_signal(
            barrier, inc=1, device_id={"rows": lax.rem(me + by, n)}, device_id_type=MESH
        )

    @pl.when(position > 0)
    def _():
        pl.semaphore_signal(
            barrier, inc=1, device_id={"pairs": position - 1}, device_id_type=MESH
        )

    @pl.when(position < n_pairs - 1)
    def _():
        pl.semaphore_signal(
            barrier, inc=1, device_id={"pairs": position + 1}, device_id_type=MESH
        )

    def all_coefs(step, shifts):
        def give(by):
            to = lax.rem(me + by, n)
            return pltpu.make_async_remote_copy(
                src_ref=partial.at[step, to // copies],
                dst_ref=arrived.at[step, me],
                send_sem=sum_sem.at[step, 0],
                recv_sem=sum_sem.at[step, 1],
                device_id={"rows": to},
                device_id_type=MESH,
            )

        def spread(by):
            to = lax.rem(own + by, half) * copies + group
            return pltpu.make_async_remote_copy(
                src_ref=coefs.at[step, own],
                dst_ref=coefs.at[step, own],
                send_sem=sum_sem.at[step, 2],
                recv_sem=sum_sem.at[step, 3],
                device_id={"rows": to},
                device_id_type=MESH,
            )

        @pl.loop(1, n)
        def _(by):
            give(by).start()

        arrived[step, me] = partial[step, own]
        some = arrived.at[step, pl.ds(0, n - 1)]
        pltpu.make_async_copy(some, some, sum_sem.at[step, 1]).wait()
        total = jnp.sum(arrived[step], axis=0)
        coefs[step, own] = turn(total, skips[step, own], shifts)

        @pl.loop(1, half)
        def _(by):
            spread(by).start()

        rest = coefs.at[step, pl.ds(0, half - 1)]
        pltpu.make_async_copy(rest, rest, sum_sem.at[step, 3]).wait()
        pltpu.make_async_copy(some, some, sum_sem.at[step, 0]).wait()
        pltpu.make_async_copy(rest, rest, sum_sem.at[step, 2]).wait()

    shifts = shifts_of(offsets, 0)

    @pl.loop(0, half)
    def _(k):
        load(k).wait()
        load(half + k).wait()
        scale = (weights[pl.ds(k, 1), :], weights[pl.ds(half + k, 1), :])
        products(data.at[k], data.at[half + k], shifts, rows, scale, partial.at[0, k])

    pl.semaphore_wait(barrier, n - 1 + not_first + 1 - is_last)
    all_coefs(0, shifts)

    def first_turn(k, upper_to, lower_to):
        rotate(
            data.at[k], data.at[half + k], moved.at[upper_to], moved.at[lower_to],
            coefs.at[0, k], shifts, rows,
        )

    out_low, out_up = 2 * half, 2 * half + 1
    low_zero = (1 - not_first) + out_low * not_first
    up_last = (2 * half - 1) * is_last + out_up * (1 - is_last)
    up_copy = pltpu.make_async_remote_copy(
        src_ref=moved.at[out_up],
        dst_ref=moved.at[0],
        send_sem=pair_sem.at[0],
        recv_sem=pair_sem.at[1],
        device_id={"pairs": lax.rem(position + 1, n_pairs)},
        device_id_type=MESH,
    )
    low_copy = pltpu.make_async_remote_copy(
        src_ref=moved.at[out_low],
        dst_ref=moved.at[2 * half - 1],
        send_sem=pair_sem.at[2],
        recv_sem=pair_sem.at[3],
        device_id={"pairs": lax.rem(position + n_pairs - 1, n_pairs)},
        device_id_type=MESH,
    )

    first_turn(half - 1, up_last, 2 * half - 2)

    @pl.when(position < n_pairs - 1)
    def _():
        up_copy.start()

    first_turn(0, not_first, low_zero)

    @pl.when(position > 0)
    def _():
        low_copy.start()

    @pl.loop(1, half - 1)
    def _(k):
        first_turn(k, k + 1, half + k - 1)

    later = shifts_of(offsets, 1)

    def second_products(k):
        products(moved.at[k], moved.at[half + k], later, rows, None, partial.at[1, k])

    @pl.loop(1, half - 1)
    def _(k):
        second_products(k)

    @pl.when(position > 0)
    def _():
        up_copy.wait_recv()
        low_copy.wait_send()

    @pl.when(position < n_pairs - 1)
    def _():
        low_copy.wait_recv()
        up_copy.wait_send()

    second_products(0)
    second_products(half - 1)
    all_coefs(1, later)

    @pl.loop(0, half)
    def _(k):
        rotate(
            moved.at[k], moved.at[half + k], data.at[k], data.at[half + k],
            coefs.at[1, k], later, rows,
        )
        store(k).start()
        store(half + k).start()
        tile = coefs[1, k] * (1.0 / (rows * n))
        power[pl.ds(k, 1), :] = tile[6:7, :]
        power[pl.ds(half + k, 1), :] = tile[7:8, :]

    @pl.loop(0, 2 * half)
    def _(block):
        store(block).wait()


def per_device(n, n_pairs, loads, col_weights, partner_offsets, skip_mask):
    rows, columns = loads.shape
    half = columns // (2 * BLOCK)
    tiles = (TILE, BLOCK)
    rotated, power = pl.pallas_call(
        functools.partial(kernel, n, n_pairs, half, rows),
        out_shape=(
            jax.ShapeDtypeStruct(loads.shape, jnp.float32),
            jax.ShapeDtypeStruct((2 * half, BLOCK), jnp.float32),
        ),
        in_specs=[
            pl.BlockSpec(memory_space=pl.ANY),
            pl.BlockSpec(memory_space=pltpu.VMEM),
            pl.BlockSpec(memory_space=pltpu.SMEM),
            pl.BlockSpec(memory_space=pltpu.SMEM),
        ],
        out_specs=(
            pl.BlockSpec(memory_space=pl.ANY),
            pl.BlockSpec(memory_space=pltpu.VMEM),
        ),
        scratch_shapes=[
            pltpu.VMEM((2 * half, rows, BLOCK), jnp.float32),
            pltpu.VMEM((2 * half + 2, rows, BLOCK), jnp.float32),
            pltpu.VMEM((STEPS, half) + tiles, jnp.float32),
            pltpu.VMEM((STEPS, n) + tiles, jnp.float32),
            pltpu.VMEM((STEPS, half) + tiles, jnp.float32),
            pltpu.SemaphoreType.DMA((2 * half,)),
            pltpu.SemaphoreType.DMA((2 * half,)),
            pltpu.SemaphoreType.DMA((STEPS, 4)),
            pltpu.SemaphoreType.DMA((4,)),
        ],
        compiler_params=pltpu.CompilerParams(
            collective_id=0, has_side_effects=True, vmem_limit_bytes=16 * 1024 * 1024
        ),
        cost_estimate=pl.CostEstimate(
            flops=60 * loads.size, bytes_accessed=8 * loads.size, transcendentals=0
        ),
    )(loads, col_weights.reshape(2 * half, BLOCK), partner_offsets, skip_mask)
    return rotated, power.reshape(columns)


def solution(mesh):
    in_specs = (P("rows", "pairs"), P("pairs"), P(), P(None, "pairs"))
    out_specs = (P("rows", "pairs"), P("pairs"))
    return jax.shard_map(
        functools.partial(per_device, mesh.shape["rows"], mesh.shape["pairs"]),
        mesh=mesh, in_specs=in_specs, out_specs=out_specs, check_vma=False,
    )
```

time: 428 us -> 44.9 us (0.10)
  waiting for transfers between devices: 189 us -> 0 us
  local copies, waits for them, and re-layouts: 137 us -> 5.56 us
  Pallas kernels: 0 us -> 38.5 us
  blocking collectives: 30.9 us -> 0 us
  other arithmetic: 26.2 us -> 0 us
  between operations: 24.6 us -> 0.65 us
  matrix products: 13.1 us -> 0 us
  starting transfers between devices: 6.11 us -> 0 us
    psum x2 -> x0, waiting for transfers between devices: 186 us -> none  [whole_gram(): return lax.psum(partial_gram, 'rows')]
    pallas_call x0 -> x1, Pallas kernels: none -> 38.5 us  [per_device(): pl.pallas_call(functools.partial(kernel, n, n_pairs, half, rows), out_sha...]
    psum x2 -> x0, local copies, waits for them, and re-layouts: 34.2 us -> none  [whole_gram(): return lax.psum(partial_gram, 'rows')]
    transpose x2 -> x0, local copies, waits for them, and re-layouts: 33.5 us -> none  [rotate_pair(): jnp.swapaxes(turn_columns(jnp.swapaxes(turned, 1, 2), cosine_values, sine...]
    psum x1 -> x0, blocking collectives: 30.9 us -> none  [per_device(): lax.psum((jnp.sum(upper_blocks * upper_blocks, axis=1), jnp.sum(lower_blo...]
    dynamic_slice x5 -> x0, local copies, waits for them, and re-layouts: 24.8 us -> none  [the longest x4 22.3 us: rotate_pair(): jnp.roll(turned[:, :half_width, half_width:], -offset, axis=2)]
    gather x16 -> x0, local copies, waits for them, and re-layouts: 19.9 us -> none  [the longest x8 11.1 us: rotate_pair(): diagonal_values = jnp.diagonal(turned, axis1=1, axis2=2)]
    dot_general x4 -> x0, matrix products: 13.1 us -> none  [the longest x2 8.4 us: whole_gram(): jnp.einsum('prc,prd->pcd', joined, joined, precision=precise, preferred_e...]
  transfers between devices with their start and end apart: 4 -> 0, of which waited for: 4 -> 0; matrix products, arithmetic and copies ran while one was open for 1% -> 0% of each run, Pallas kernels for 0% -> 0%
where the time goes in v1:
time: 44.9 us; the launch traced here: 44.7 us
  Pallas kernels  38.5 us (86%)
  local copies, waits for them, and re-layouts  5.56 us (12%)
  between operations  0.65 us (1%)
    pallas_call x1, Pallas kernels, per_device(): pl.pallas_call(functools.partial(kernel, n, n_pairs, half, rows), out_sha...  38.5 us
    unnamed x10, local copies, waits for them, and re-layouts  5.56 us

profile of v1, /device:TPU:0, one launch (start us, length us, event | category | flops | bytes accessed | tf_op | source)
XLA Modules:
  0.0 44.7 jit_solution(2027690260190567600)
XLA Ops:
  0.6 0.0 copy-start
  0.6 1.6 %copy-done = f32[256,2048]{1,0:T(8,128)S(1)} copy-done((f32[256,2048]{1,0:T(8,128)S(1)}, f32[256,2048]{1,0:T(8,128)}, u32[]{:S(2)}) %copy-start) | copy-done | bytes 2097176
  2.2 0.0 copy-start.1
  2.2 0.7 %copy-done.1 = f32[2048]{0:T(1024)S(1)} copy-done((f32[2048]{0:T(1024)S(1)}, f32[2048]{0:T(1024)}, u32[]{:S(2)}) %copy-start.1) | copy-done | bytes 8216
  2.9 0.0 copy-start.2
  2.9 0.7 %copy-done.2 = s32[2,2]{1,0:T(2,128)S(1)} copy-done((s32[2,2]{1,0:T(2,128)S(1)}, s32[2,2]{1,0:T(2,128)}, u32[]{:S(2)}) %copy-start.2) | copy-done | bytes 40
  3.6 0.0 copy-start.3
  3.6 0.7 %copy-done.3 = s32[2,8]{1,0:T(2,128)S(1)} copy-done((s32[2,8]{1,0:T(2,128)S(1)}, s32[2,8]{1,0:T(2,128)}, u32[]{:S(2)}) %copy-start.3) | copy-done | bytes 88
  4.3 38.5 %shard_map.59 = (f32[256,2048]{1,0:T(8,128)S(1)}, f32[16,128]{1,0:T(8,128)S(1)}) custom-call(f32[256,2048]{1,0:T(8,128)S(1)} %copy-done, f32[16,128]{1,0:T(8,128)S(1)} %bitcast.2, s32[2,2]{1,0:T(2,128)S(1)} %copy-done.2, s32[2,8]{1,0:T(2,128)S(1)} %copy-done.3), custom_call_target="tpu_custom_call" | custom-call | flops 31457280 | bytes 4194304 | tf_op jit(solution)/shard_map/pallas_call | solution.py:292
  42.8 1.3 %copy.8 = f32[256,2048]{1,0:T(8,128)} copy(f32[256,2048]{1,0:T(8,128)S(1)} %get-tuple-element.8) | data formatting | bytes 4194304
  44.1 0.6 %copy.9 = f32[2048]{0:T(1024)} copy(f32[2048]{0:T(1024)S(1)} %bitcast.3) | data formatting | bytes 16384
Async XLA Ops:
  0.6 1.6 %copy-start = (f32[256,2048]{1,0:T(8,128)S(1)}, f32[256,2048]{1,0:T(8,128)}, u32[]{:S(2)}) copy-start(f32[256,2048]{1,0:T(8,128)} %loads.1) | copy-start | bytes 6291460
  2.2 0.7 %copy-start.1 = (f32[2048]{0:T(1024)S(1)}, f32[2048]{0:T(1024)}, u32[]{:S(2)}) copy-start(f32[2048]{0:T(1024)} %param.5) | copy-start | bytes 24580
  2.9 0.7 %copy-start.2 = (s32[2,2]{1,0:T(2,128)S(1)}, s32[2,2]{1,0:T(2,128)}, u32[]{:S(2)}) copy-start(s32[2,2]{1,0:T(2,128)} %offsets.1) | copy-start | bytes 52
  3.6 0.7 %copy-start.3 = (s32[2,8]{1,0:T(2,128)S(1)}, s32[2,8]{1,0:T(2,128)}, u32[]{:S(2)}) copy-start(s32[2,8]{1,0:T(2,128)} %skips.1) | copy-start | bytes 196

commit v2 on v1

--- a/solution.py
+++ b/solution.py
@@ -9,7 +9,7 @@
 BLOCK = 128
 STEPS = 2
 TILE = 8
-CHUNK = 64
+CHUNK = 32
 MESH = pl.DeviceIdType.MESH
 
 
@@ -44,7 +44,7 @@
         return tuple(total + fold(a * b) for total, (a, b) in zip(sums, pairs))
 
     zero = jnp.zeros((TILE, BLOCK), jnp.float32)
-    sums = lax.fori_loop(0, rows // CHUNK, body, (zero,) * 7)
+    sums = lax.fori_loop(0, rows // CHUNK, body, (zero,) * 7, unroll=True)
     for at, total in enumerate(sums):
         partial[pl.ds(at, 1), :] = jnp.sum(total, axis=0, keepdims=True)
     partial[pl.ds(7, 1), :] = jnp.zeros((1, BLOCK), jnp.float32)
@@ -101,14 +101,14 @@
         new_lower[spot, :] = rolled(sum(f * x for f, x in zip(low, parts)), back)
         return carry
 
-    lax.fori_loop(0, rows // CHUNK, body, 0)
+    lax.fori_loop(0, rows // CHUNK, body, 0, unroll=True)
 
 
 def kernel(
     n, n_pairs, half, rows,
-    loads, weights, offsets, skips,
+    loads, weights_in, offsets_in, skips_in,
     rotated, power,
-    data, moved, partial, arrived, coefs,
+    weights, offsets, skips, small_sem, data, moved, partial, arrived, coefs,
     load_sem, store_sem, sum_sem, pair_sem,
 ):
     me, position = lax.axis_index("rows"), lax.axis_index("pairs")
@@ -125,6 +125,13 @@
         columns = pl.ds(pl.multiple_of(block * BLOCK, BLOCK), BLOCK)
         return pltpu.make_async_copy(data.at[block], rotated.at[:, columns], store_sem.at[block])
 
+    small = [
+        pltpu.make_async_copy(offsets_in, offsets, small_sem.at[0]),
+        pltpu.make_async_copy(weights_in, weights, small_sem.at[1]),
+        pltpu.make_async_copy(skips_in, skips, small_sem.at[2]),
+    ]
+    for copy in small:
+        copy.start()
     for k in range(half):
         load(k).start()
         load(half + k).start()
@@ -191,6 +198,8 @@
         pltpu.make_async_copy(some, some, sum_sem.at[step, 0]).wait()
         pltpu.make_async_copy(rest, rest, sum_sem.at[step, 2]).wait()
 
+    for copy in small:
+        copy.wait()
     shifts = shifts_of(offsets, 0)
 
     @pl.loop(0, half)
@@ -296,16 +305,20 @@
             jax.ShapeDtypeStruct((2 * half, BLOCK), jnp.float32),
         ),
         in_specs=[
-            pl.BlockSpec(memory_space=pl.ANY),
-            pl.BlockSpec(memory_space=pltpu.VMEM),
-            pl.BlockSpec(memory_space=pltpu.SMEM),
-            pl.BlockSpec(memory_space=pltpu.SMEM),
+            pl.BlockSpec(memory_space=pltpu.HBM),
+            pl.BlockSpec(memory_space=pltpu.HBM),
+            pl.BlockSpec(memory_space=pltpu.HBM),
+            pl.BlockSpec(memory_space=pltpu.HBM),
         ],
         out_specs=(
             pl.BlockSpec(memory_space=pl.ANY),
             pl.BlockSpec(memory_space=pltpu.VMEM),
         ),
         scratch_shapes=[
+            pltpu.VMEM((2 * half, BLOCK), jnp.float32),
+            pltpu.SMEM(partner_offsets.shape, jnp.int32),
+            pltpu.SMEM(skip_mask.shape, jnp.int32),
+            pltpu.SemaphoreType.DMA((3,)),
             pltpu.VMEM((2 * half, rows, BLOCK), jnp.float32),
             pltpu.VMEM((2 * half + 2, rows, BLOCK), jnp.float32),
             pltpu.VMEM((STEPS, half) + tiles, jnp.float32),
@@ -317,7 +330,7 @@
             pltpu.SemaphoreType.DMA((4,)),
         ],
         compiler_params=pltpu.CompilerParams(
-            collective_id=0, has_side_effects=True, vmem_limit_bytes=16 * 1024 * 1024
+            collective_id=0, has_side_effects=True, vmem_limit_bytes=60 * 1024 * 1024
         ),
         cost_estimate=pl.CostEstimate(
             flops=60 * loads.size, bytes_accessed=8 * loads.size, transcendentals=0

time: 44.9 us -> 37.3 us (0.83)
  Pallas kernels: 38.5 us -> 32.7 us
  local copies, waits for them, and re-layouts: 5.56 us -> 3.74 us
    pallas_call x1, Pallas kernels: 38.5 us -> 32.7 us  [per_device(): pl.pallas_call(functools.partial(kernel, n, n_pairs, half, rows), out_sha...]
    unnamed x10 -> x4, local copies, waits for them, and re-layouts: 5.56 us -> 3.74 us
where the time goes in v2:
time: 37.3 us; the launch traced here: 37.1 us
  Pallas kernels  32.7 us (88%)
  local copies, waits for them, and re-layouts  3.74 us (10%)
  between operations  0.65 us (2%)
    pallas_call x1, Pallas kernels, per_device(): pl.pallas_call(functools.partial(kernel, n, n_pairs, half, rows), out_sha...  32.7 us
    unnamed x4, local copies, waits for them, and re-layouts  3.74 us

profile of v2, /device:TPU:0, one launch (start us, length us, event | category | flops | bytes accessed | tf_op | source)
XLA Modules:
  0.0 37.1 jit_solution(10032561200159084735)
XLA Ops:
  0.6 32.7 %shard_map.59 = (f32[256,2048]{1,0:T(8,128)}, f32[16,128]{1,0:T(8,128)}) custom-call(f32[256,2048]{1,0:T(8,128)} %loads.1, f32[16,128]{1,0:T(8,128)} %bitcast.2, s32[2,2]{1,0:T(2,128)} %offsets_in.1, s32[2,8]{1,0:T(2,128)} %skips_in.1), custom_call_target="tpu_custom_call" | custom-call | flops 31457280 | bytes 4194304 | tf_op jit(solution)/shard_map/pallas_call | solution.py:301
  33.4 0.0 copy-start
  33.4 3.1 %copy.8 = f32[256,2048]{1,0:T(8,128)} copy(f32[256,2048]{1,0:T(8,128)} %get-tuple-element.8) | data formatting | bytes 4194304
  36.5 0.0 copy-done
  36.5 0.6 %copy.9 = f32[2048]{0:T(1024)} copy(f32[2048]{0:T(1024)S(1)} %bitcast.3) | data formatting | bytes 16384
Async XLA Ops:
  33.4 3.2 %copy-start = (f32[16,128]{1,0:T(8,128)S(1)}, f32[16,128]{1,0:T(8,128)}, u32[]{:S(2)}) copy-start(f32[16,128]{1,0:T(8,128)} %get-tuple-element.5) | copy-start | bytes 24580

commit v3 on v2

--- a/solution.py
+++ b/solution.py
@@ -104,12 +104,16 @@
     lax.fori_loop(0, rows // CHUNK, body, 0, unroll=True)
 
 
-def kernel(
+def column_block(array, block):
+    return array.at[:, pl.ds(pl.multiple_of(block * BLOCK, BLOCK), BLOCK)]
+
+
+def turning_kernel(
     n, n_pairs, half, rows,
     loads, weights_in, offsets_in, skips_in,
-    rotated, power,
-    weights, offsets, skips, small_sem, data, moved, partial, arrived, coefs,
-    load_sem, store_sem, sum_sem, pair_sem,
+    moved_out, coefs_out,
+    weights, offsets, skips, data, moved, partial, arrived, coefs,
+    small_sem, load_sem, store_sem, give_sem, arrive_sem, spread_sem, coef_sem, pair_sem,
 ):
     me, position = lax.axis_index("rows"), lax.axis_index("pairs")
     copies = n // half
@@ -118,12 +122,12 @@
     is_last = (position + 1) // n_pairs
 
     def load(block):
-        columns = pl.ds(pl.multiple_of(block * BLOCK, BLOCK), BLOCK)
-        return pltpu.make_async_copy(loads.at[:, columns], data.at[block], load_sem.at[block])
+        return pltpu.make_async_copy(
+            column_block(loads, block), data.at[block], load_sem.at[block]
+        )
 
     def store(block):
-        columns = pl.ds(pl.multiple_of(block * BLOCK, BLOCK), BLOCK)
-        return pltpu.make_async_copy(data.at[block], rotated.at[:, columns], store_sem.at[block])
+        return pltpu.make_async_copy(moved.at[block], moved_out.at[block], store_sem.at[block])
 
     small = [
         pltpu.make_async_copy(offsets_in, offsets, small_sem.at[0]),
@@ -156,63 +160,83 @@
             barrier, inc=1, device_id={"pairs": position + 1}, device_id_type=MESH
         )
 
-    def all_coefs(step, shifts):
-        def give(by):
-            to = lax.rem(me + by, n)
-            return pltpu.make_async_remote_copy(
-                src_ref=partial.at[step, to // copies],
-                dst_ref=arrived.at[step, me],
-                send_sem=sum_sem.at[step, 0],
-                recv_sem=sum_sem.at[step, 1],
+    def give(step, k):
+        @pl.loop(0, copies)
+        def _(at):
+            to = k * copies + at
+
+            @pl.when(to != me)
+            def _():
+                pltpu.make_async_remote_copy(
+                    src_ref=partial.at[step, k],
+                    dst_ref=arrived.at[step, me],
+                    send_sem=give_sem.at[step],
+                    recv_sem=arrive_sem.at[step],
+                    device_id={"rows": to},
+                    device_id_type=MESH,
+                ).start()
+
+            @pl.when(to == me)
+            def _():
+                arrived[step, me] = partial[step, k]
+
+    def own_coefs(step, shifts):
+        some = arrived.at[step, pl.ds(0, n - 1)]
+        pltpu.make_async_copy(some, some, arrive_sem.at[step]).wait()
+        total = jnp.sum(arrived[step], axis=0)
+        coefs[step, own] = turn(total, skips[step, own], shifts)
+        target = coefs.at[0] if step == 0 else coefs_out
+
+        @pl.loop(1, half)
+        def _(by):
+            to = lax.rem(own + by, half) * copies + group
+            pltpu.make_async_remote_copy(
+                src_ref=coefs.at[step, own],
+                dst_ref=target.at[own],
+                send_sem=spread_sem.at[step],
+                recv_sem=coef_sem.at[step, own],
                 device_id={"rows": to},
                 device_id_type=MESH,
-            )
-
-        def spread(by):
-            to = lax.rem(own + by, half) * copies + group
-            return pltpu.make_async_remote_copy(
-                src_ref=coefs.at[step, own],
-                dst_ref=coefs.at[step, own],
-                send_sem=sum_sem.at[step, 2],
-                recv_sem=sum_sem.at[step, 3],
-                device_id={"rows": to},
-                device_id_type=MESH,
-            )
-
-        @pl.loop(1, n)
-        def _(by):
-            give(by).start()
-
-        arrived[step, me] = partial[step, own]
-        some = arrived.at[step, pl.ds(0, n - 1)]
-        pltpu.make_async_copy(some, some, sum_sem.at[step, 1]).wait()
-        total = jnp.sum(arrived[step], axis=0)
-        coefs[step, own] = turn(total, skips[step, own], shifts)
-
-        @pl.loop(1, half)
-        def _(by):
-            spread(by).start()
-
-        rest = coefs.at[step, pl.ds(0, half - 1)]
-        pltpu.make_async_copy(rest, rest, sum_sem.at[step, 3]).wait()
-        pltpu.make_async_copy(some, some, sum_sem.at[step, 0]).wait()
-        pltpu.make_async_copy(rest, rest, sum_sem.at[step, 2]).wait()
+            ).start()
+
+    def wait_coefs(step, k):
+        tile = coefs.at[step, k]
+
+        @pl.when(k != own)
+        def _():
+            pltpu.make_async_copy(tile, tile, coef_sem.at[step, k]).wait()
 
     for copy in small:
         copy.wait()
     shifts = shifts_of(offsets, 0)
 
-    @pl.loop(0, half)
-    def _(k):
+    def first_products(k):
         load(k).wait()
         load(half + k).wait()
         scale = (weights[pl.ds(k, 1), :], weights[pl.ds(half + k, 1), :])
         products(data.at[k], data.at[half + k], shifts, rows, scale, partial.at[0, k])
 
+    early = half // 2
+
+    @pl.loop(0, early)
+    def _(k):
+        first_products(k)
+
     pl.semaphore_wait(barrier, n - 1 + not_first + 1 - is_last)
-    all_coefs(0, shifts)
+
+    @pl.loop(0, early)
+    def _(k):
+        give(0, k)
+
+    @pl.loop(early, half)
+    def _(k):
+        first_products(k)
+        give(0, k)
+
+    own_coefs(0, shifts)
 
     def first_turn(k, upper_to, lower_to):
+        wait_coefs(0, k)
         rotate(
             data.at[k], data.at[half + k], moved.at[upper_to], moved.at[lower_to],
             coefs.at[0, k], shifts, rows,
@@ -257,37 +281,87 @@
     later = shifts_of(offsets, 1)
 
     def second_products(k):
-        products(moved.at[k], moved.at[half + k], later, rows, None, partial.at[1, k])
-
-    @pl.loop(1, half - 1)
-    def _(k):
-        second_products(k)
-
-    @pl.when(position > 0)
-    def _():
-        up_copy.wait_recv()
-        low_copy.wait_send()
-
-    @pl.when(position < n_pairs - 1)
-    def _():
-        low_copy.wait_recv()
-        up_copy.wait_send()
-
-    second_products(0)
-    second_products(half - 1)
-    all_coefs(1, later)
-
-    @pl.loop(0, half)
-    def _(k):
-        rotate(
-            moved.at[k], moved.at[half + k], data.at[k], data.at[half + k],
-            coefs.at[1, k], later, rows,
-        )
         store(k).start()
         store(half + k).start()
-        tile = coefs[1, k] * (1.0 / (rows * n))
-        power[pl.ds(k, 1), :] = tile[6:7, :]
-        power[pl.ds(half + k, 1), :] = tile[7:8, :]
+        products(moved.at[k], moved.at[half + k], later, rows, None, partial.at[1, k])
+        give(1, k)
+
+    @pl.loop(1, half - 1)
+    def _(k):
+        second_products(k)
+
+    @pl.when(position > 0)
+    def _():
+        up_copy.wait_recv()
+
+    second_products(0)
+
+    @pl.when(position < n_pairs - 1)
+    def _():
+        low_copy.wait_recv()
+
+    second_products(half - 1)
+    own_coefs(1, later)
+    own_copy = pltpu.make_async_copy(coefs.at[1, own], coefs_out.at[own], coef_sem.at[1, own])
+    own_copy.start()
+
+    @pl.when(position > 0)
+    def _():
+        low_copy.wait_send()
+
+    @pl.when(position < n_pairs - 1)
+    def _():
+        up_copy.wait_send()
+
+    for step in range(STEPS):
+        some = arrived.at[step, pl.ds(0, n - 1)]
+        pltpu.make_async_copy(some, some, give_sem.at[step]).wait()
+        rest = coefs.at[step, pl.ds(0, half - 1)]
+        pltpu.make_async_copy(rest, rest, spread_sem.at[step]).wait()
+
+    @pl.loop(0, 2 * half)
+    def _(block):
+        store(block).wait()
+
+    own_copy.wait()
+
+    @pl.loop(0, half)
+    def _(k):
+        wait_coefs(1, k)
+
+
+def last_kernel(
+    scale, half, rows,
+    moved, coefs_in, offsets,
+    rotated, power,
+    data, coefs, load_sem, coef_sem, store_sem,
+):
+    def load(block):
+        return pltpu.make_async_copy(moved.at[block], data.at[block], load_sem.at[block])
+
+    def store(block):
+        return pltpu.make_async_copy(
+            data.at[block], column_block(rotated, block), store_sem.at[block]
+        )
+
+    coef_copy = pltpu.make_async_copy(coefs_in, coefs, coef_sem)
+    coef_copy.start()
+    for k in range(half):
+        load(k).start()
+        load(half + k).start()
+    shifts = shifts_of(offsets, STEPS - 1)
+    coef_copy.wait()
+
+    @pl.loop(0, half)
+    def _(k):
+        load(k).wait()
+        load(half + k).wait()
+        upper, lower = data.at[k], data.at[half + k]
+        rotate(upper, lower, upper, lower, coefs.at[k], shifts, rows)
+        store(k).start()
+        store(half + k).start()
+        power[pl.ds(k, 1), :] = coefs[k, pl.ds(6, 1), :] * scale
+        power[pl.ds(half + k, 1), :] = coefs[k, pl.ds(7, 1), :] * scale
 
     @pl.loop(0, 2 * half)
     def _(block):
@@ -298,44 +372,62 @@
     rows, columns = loads.shape
     half = columns // (2 * BLOCK)
     tiles = (TILE, BLOCK)
-    rotated, power = pl.pallas_call(
-        functools.partial(kernel, n, n_pairs, half, rows),
+    hbm = pl.BlockSpec(memory_space=pltpu.HBM)
+    dma = pltpu.SemaphoreType.DMA
+    limit = 60 * 1024 * 1024
+    moved, coefs = pl.pallas_call(
+        functools.partial(turning_kernel, n, n_pairs, half, rows),
         out_shape=(
-            jax.ShapeDtypeStruct(loads.shape, jnp.float32),
-            jax.ShapeDtypeStruct((2 * half, BLOCK), jnp.float32),
+            jax.ShapeDtypeStruct((2 * half, rows, BLOCK), jnp.float32),
+            jax.ShapeDtypeStruct((half,) + tiles, jnp.float32),
         ),
-        in_specs=[
-            pl.BlockSpec(memory_space=pltpu.HBM),
-            pl.BlockSpec(memory_space=pltpu.HBM),
-            pl.BlockSpec(memory_space=pltpu.HBM),
-            pl.BlockSpec(memory_space=pltpu.HBM),
-        ],
-        out_specs=(
-            pl.BlockSpec(memory_space=pl.ANY),
-            pl.BlockSpec(memory_space=pltpu.VMEM),
-        ),
+        in_specs=[hbm] * 4,
+        out_specs=(hbm, hbm),
         scratch_shapes=[
             pltpu.VMEM((2 * half, BLOCK), jnp.float32),
             pltpu.SMEM(partner_offsets.shape, jnp.int32),
             pltpu.SMEM(skip_mask.shape, jnp.int32),
-            pltpu.SemaphoreType.DMA((3,)),
             pltpu.VMEM((2 * half, rows, BLOCK), jnp.float32),
             pltpu.VMEM((2 * half + 2, rows, BLOCK), jnp.float32),
             pltpu.VMEM((STEPS, half) + tiles, jnp.float32),
             pltpu.VMEM((STEPS, n) + tiles, jnp.float32),
             pltpu.VMEM((STEPS, half) + tiles, jnp.float32),
-            pltpu.SemaphoreType.DMA((2 * half,)),
-            pltpu.SemaphoreType.DMA((2 * half,)),
-            pltpu.SemaphoreType.DMA((STEPS, 4)),
-            pltpu.SemaphoreType.DMA((4,)),
+            dma((3,)),
+            dma((2 * half,)),
+            dma((2 * half,)),
+            dma((STEPS,)),
+            dma((STEPS,)),
+            dma((STEPS,)),
+            dma((STEPS, half)),
+            dma((4,)),
         ],
         compiler_params=pltpu.CompilerParams(
-            collective_id=0, has_side_effects=True, vmem_limit_bytes=60 * 1024 * 1024
+            collective_id=0, has_side_effects=True, vmem_limit_bytes=limit
         ),
         cost_estimate=pl.CostEstimate(
             flops=60 * loads.size, bytes_accessed=8 * loads.size, transcendentals=0
         ),
     )(loads, col_weights.reshape(2 * half, BLOCK), partner_offsets, skip_mask)
+    rotated, power = pl.pallas_call(
+        functools.partial(last_kernel, 1.0 / (rows * n), half, rows),
+        out_shape=(
+            jax.ShapeDtypeStruct(loads.shape, jnp.float32),
+            jax.ShapeDtypeStruct((2 * half, BLOCK), jnp.float32),
+        ),
+        in_specs=[hbm, hbm, pl.BlockSpec(memory_space=pltpu.SMEM)],
+        out_specs=(hbm, pl.BlockSpec(memory_space=pltpu.VMEM)),
+        scratch_shapes=[
+            pltpu.VMEM((2 * half, rows, BLOCK), jnp.float32),
+            pltpu.VMEM((half,) + tiles, jnp.float32),
+            dma((2 * half,)),
+            dma(()),
+            dma((2 * half,)),
+        ],
+        compiler_params=pltpu.CompilerParams(vmem_limit_bytes=limit),
+        cost_estimate=pl.CostEstimate(
+            flops=20 * loads.size, bytes_accessed=8 * loads.size, transcendentals=0
+        ),
+    )(moved, coefs, partner_offsets)
     return rotated, power.reshape(columns)
 
 

time: 37.3 us -> 35.9 us (0.962)
  local copies, waits for them, and re-layouts: 3.74 us -> 0 us
  Pallas kernels: 32.7 us -> 35.1 us
    unnamed x4 -> x0, local copies, waits for them, and re-layouts: 3.74 us -> none
    pallas_call x1 -> x2, Pallas kernels: 32.7 us -> 35.1 us  [the longest x1 29.1 us: per_device(): pl.pallas_call(functools.partial(turning_kernel, n, n_pairs, half, rows),...]
where the time goes in v3:
time: 35.9 us; the launch traced here: 35.7 us
  Pallas kernels  35.1 us (98%)
  between operations  0.64 us (2%)
    pallas_call x1, Pallas kernels, per_device(): pl.pallas_call(functools.partial(turning_kernel, n, n_pairs, half, rows),...  29.1 us
    pallas_call x1, Pallas kernels, per_device(): pl.pallas_call(functools.partial(last_kernel, 1.0 / (rows * n), half, row...  5.99 us

profile of v3, /device:TPU:0, one launch (start us, length us, event | category | flops | bytes accessed | tf_op | source)
XLA Modules:
  0.0 35.7 jit_solution(5725502232258983883)
XLA Ops:
  0.6 29.1 %shard_map.59 = (f32[16,256,128]{2,1,0:T(8,128)}, f32[8,8,128]{2,1,0:T(8,128)}) custom-call(f32[256,2048]{1,0:T(8,128)} %loads.1, f32[16,128]{1,0:T(8,128)} %bitcast.2, s32[2,2]{1,0:T(2,128)} %offsets.1, s32[2,8]{1,0:T(2,128)} %skips_in.1), custom_call_target="tpu_custom_call" | custom-call | flops 31457280 | bytes 4194304 | tf_op jit(solution)/shard_map/pallas_call | solution.py:378
  29.7 6.0 %shard_map.60 = (f32[256,2048]{1,0:T(8,128)}, f32[16,128]{1,0:T(8,128)}) custom-call(f32[16,256,128]{2,1,0:T(8,128)} %get-tuple-element.6.moved, f32[8,8,128]{2,1,0:T(8,128)} %get-tuple-element.7.coefs_in, s32[2,2]{1,0:T(2,128)} %offsets.1), custom_call_target="tpu_custom_call" | custom-call | flops 10485760 | bytes 4194304 | tf_op jit(solution)/shard_map/pallas_call | solution.py:411

commit v4 on v3

--- a/solution.py
+++ b/solution.py
@@ -29,22 +29,67 @@
     return to_first, to_second, between, second
 
 
-def products(upper, lower, shifts, rows, weights, partial):
-    to_first, to_second, between, _ = shifts
-
-    def body(at, sums):
-        spot = pl.ds(pl.multiple_of(at * CHUNK, CHUNK), CHUNK)
+def permutations(shifts, target):
+    to_first, to_second, between, back = shifts
+    shape = (2 * BLOCK, BLOCK)
+    apart = lax.broadcasted_iota(jnp.int32, shape, 0) - lax.broadcasted_iota(jnp.int32, shape, 1)
+    for at, shift in enumerate((between, to_first, to_second, back)):
+        hit = lax.rem(apart + (shift + BLOCK), BLOCK) == 0
+        target[:, at * BLOCK : (at + 1) * BLOCK] = jnp.where(hit, 1.0, 0.0).astype(jnp.bfloat16)
+
+
+def put_split(x, target, spot):
+    high = x.astype(jnp.bfloat16)
+    target[spot, :BLOCK] = high
+    target[spot, BLOCK:] = (x - high.astype(jnp.float32)).astype(jnp.bfloat16)
+
+
+def times(x, matrix):
+    return jnp.dot(x, matrix, preferred_element_type=jnp.float32)
+
+
+def chunks(rows, body, carry):
+    def step(at, carry):
+        return body(pl.ds(pl.multiple_of(at * CHUNK, CHUNK), CHUNK), carry)
+
+    return lax.fori_loop(0, rows // CHUNK, step, carry, unroll=True)
+
+
+zero_tile = (TILE, BLOCK)
+
+
+def roll_all(upper, lower, perms, splits, turned, rows, weights):
+    def body(spot, sums):
         u, l = upper[spot, :], lower[spot, :]
         if weights is not None:
             u, l = u * weights[0], l * weights[1]
             upper[spot, :] = u
-            lower[spot, :] = l
-        lp, ud, ld = rolled(l, to_first), rolled(u, between), rolled(l, to_second)
-        pairs = ((u, u), (lp, lp), (u, lp), (u, ud), (u, ld), (lp, ud), (lp, ld))
+        put_split(u, splits.at[0], spot)
+        put_split(l, splits.at[1], spot)
+        return sums[0] + fold(u * u), sums[1] + fold(l * l)
+
+    zero = jnp.zeros(zero_tile, jnp.float32)
+    sums = chunks(rows, body, (zero, zero))
+    turned[:, :BLOCK] = times(splits[0], perms[:, :BLOCK])
+    turned[:, BLOCK:] = times(splits[1], perms[:, BLOCK : 3 * BLOCK])
+    return sums
+
+
+def parts_of(upper, turned, spot):
+    lp, ld = turned[spot, BLOCK : 2 * BLOCK], turned[spot, 2 * BLOCK :]
+    return upper[spot, :], lp, turned[spot, :BLOCK], ld
+
+
+def products(upper, lower, perms, splits, turned, rows, weights, partial):
+    squares = roll_all(upper, lower, perms, splits, turned, rows, weights)
+
+    def body(spot, sums):
+        u, lp, ud, ld = parts_of(upper, turned, spot)
+        pairs = ((u, lp), (u, ud), (u, ld), (lp, ud), (lp, ld))
         return tuple(total + fold(a * b) for total, (a, b) in zip(sums, pairs))
 
-    zero = jnp.zeros((TILE, BLOCK), jnp.float32)
-    sums = lax.fori_loop(0, rows // CHUNK, body, (zero,) * 7, unroll=True)
+    zero = jnp.zeros(zero_tile, jnp.float32)
+    sums = squares + chunks(rows, body, (zero,) * 5)
     for at, total in enumerate(sums):
         partial[pl.ds(at, 1), :] = jnp.sum(total, axis=0, keepdims=True)
     partial[pl.ds(7, 1), :] = jnp.zeros((1, BLOCK), jnp.float32)
@@ -67,9 +112,10 @@
 
 
 def turn(total, skip, shifts):
-    _, _, between, back = shifts
+    to_first, _, between, back = shifts
     row = [jnp.broadcast_to(total[at : at + 1, :], (TILE, BLOCK)) for at in range(7)]
     a, b, g, u_ud, u_ld, l_ud, l_ld = row
+    b = rolled(b, to_first)
     keep = jnp.full((TILE, BLOCK), skip, jnp.int32) == 0
     c, s = angle(a, b, g)
     c, s = jnp.where(keep, c, 1.0), jnp.where(keep, s, 0.0)
@@ -86,22 +132,20 @@
     return tile
 
 
-def rotate(upper, lower, new_upper, new_lower, coefs, shifts, rows):
-    to_first, to_second, between, back = shifts
+def rotate(upper, new_upper, new_lower, coefs, perms, splits, turned, rows):
     tile = coefs[...]
     c, s, cd, sd, c2, s2 = (tile[at : at + 1, :] for at in range(6))
     up = (c2 * c, -c2 * s, -s2 * sd, -s2 * cd)
     low = (s2 * c, -s2 * s, c2 * sd, c2 * cd)
 
-    def body(at, carry):
-        spot = pl.ds(pl.multiple_of(at * CHUNK, CHUNK), CHUNK)
-        u, l = upper[spot, :], lower[spot, :]
-        parts = (u, rolled(l, to_first), rolled(u, between), rolled(l, to_second))
+    def body(spot, carry):
+        parts = parts_of(upper, turned, spot)
         new_upper[spot, :] = sum(f * x for f, x in zip(up, parts))
-        new_lower[spot, :] = rolled(sum(f * x for f, x in zip(low, parts)), back)
+        put_split(sum(f * x for f, x in zip(low, parts)), splits.at[1], spot)
         return carry
 
-    lax.fori_loop(0, rows // CHUNK, body, 0, unroll=True)
+    chunks(rows, body, 0)
+    new_lower[...] = times(splits[1], perms[:, 3 * BLOCK :])
 
 
 def column_block(array, block):
@@ -112,7 +156,7 @@
     n, n_pairs, half, rows,
     loads, weights_in, offsets_in, skips_in,
     moved_out, coefs_out,
-    weights, offsets, skips, data, moved, partial, arrived, coefs,
+    weights, offsets, skips, data, moved, partial, arrived, coefs, perms, splits, turned,
     small_sem, load_sem, store_sem, give_sem, arrive_sem, spread_sem, coef_sem, pair_sem,
 ):
     me, position = lax.axis_index("rows"), lax.axis_index("pairs")
@@ -209,12 +253,17 @@
     for copy in small:
         copy.wait()
     shifts = shifts_of(offsets, 0)
+    later = shifts_of(offsets, 1)
+    permutations(shifts, perms.at[0])
 
     def first_products(k):
         load(k).wait()
         load(half + k).wait()
         scale = (weights[pl.ds(k, 1), :], weights[pl.ds(half + k, 1), :])
-        products(data.at[k], data.at[half + k], shifts, rows, scale, partial.at[0, k])
+        products(
+            data.at[k], data.at[half + k], perms.at[0], splits.at[k], turned.at[k],
+            rows, scale, partial.at[0, k],
+        )
 
     early = half // 2
 
@@ -233,13 +282,14 @@
         first_products(k)
         give(0, k)
 
+    permutations(later, perms.at[1])
     own_coefs(0, shifts)
 
     def first_turn(k, upper_to, lower_to):
         wait_coefs(0, k)
         rotate(
-            data.at[k], data.at[half + k], moved.at[upper_to], moved.at[lower_to],
-            coefs.at[0, k], shifts, rows,
+            data.at[k], moved.at[upper_to], moved.at[lower_to], coefs.at[0, k],
+            perms.at[0], splits.at[k], turned.at[k], rows,
         )
 
     out_low, out_up = 2 * half, 2 * half + 1
@@ -278,12 +328,13 @@
     def _(k):
         first_turn(k, k + 1, half + k - 1)
 
-    later = shifts_of(offsets, 1)
-
     def second_products(k):
         store(k).start()
         store(half + k).start()
-        products(moved.at[k], moved.at[half + k], later, rows, None, partial.at[1, k])
+        products(
+            moved.at[k], moved.at[half + k], perms.at[1], splits.at[k], turned.at[k],
+            rows, None, partial.at[1, k],
+        )
         give(1, k)
 
     @pl.loop(1, half - 1)
@@ -334,7 +385,7 @@
     scale, half, rows,
     moved, coefs_in, offsets,
     rotated, power,
-    data, coefs, load_sem, coef_sem, store_sem,
+    data, coefs, perms, splits, turned, load_sem, coef_sem, store_sem,
 ):
     def load(block):
         return pltpu.make_async_copy(moved.at[block], data.at[block], load_sem.at[block])
@@ -349,7 +400,7 @@
     for k in range(half):
         load(k).start()
         load(half + k).start()
-    shifts = shifts_of(offsets, STEPS - 1)
+    permutations(shifts_of(offsets, STEPS - 1), perms)
     coef_copy.wait()
 
     @pl.loop(0, half)
@@ -357,7 +408,10 @@
         load(k).wait()
         load(half + k).wait()
         upper, lower = data.at[k], data.at[half + k]
-        rotate(upper, lower, upper, lower, coefs.at[k], shifts, rows)
+        roll_all(upper, lower, perms, splits.at[k], turned.at[k], rows, None)
+        rotate(
+            upper, upper, lower, coefs.at[k], perms, splits.at[k], turned.at[k], rows
+        )
         store(k).start()
         store(half + k).start()
         power[pl.ds(k, 1), :] = coefs[k, pl.ds(6, 1), :] * scale
@@ -392,6 +446,9 @@
             pltpu.VMEM((STEPS, half) + tiles, jnp.float32),
             pltpu.VMEM((STEPS, n) + tiles, jnp.float32),
             pltpu.VMEM((STEPS, half) + tiles, jnp.float32),
+            pltpu.VMEM((STEPS, 2 * BLOCK, 4 * BLOCK), jnp.bfloat16),
+            pltpu.VMEM((half, 2, rows, 2 * BLOCK), jnp.bfloat16),
+            pltpu.VMEM((half, rows, 3 * BLOCK), jnp.float32),
             dma((3,)),
             dma((2 * half,)),
             dma((2 * half,)),
@@ -419,6 +476,9 @@
         scratch_shapes=[
             pltpu.VMEM((2 * half, rows, BLOCK), jnp.float32),
             pltpu.VMEM((half,) + tiles, jnp.float32),
+            pltpu.VMEM((2 * BLOCK, 4 * BLOCK), jnp.bfloat16),
+            pltpu.VMEM((half, 2, rows, 2 * BLOCK), jnp.bfloat16),
+            pltpu.VMEM((half, rows, 3 * BLOCK), jnp.float32),
             dma((2 * half,)),
             dma(()),
             dma((2 * half,)),

time: 35.9 us -> 37.2 us (1.036)
  Pallas kernels: 35.1 us -> 36.4 us
    pallas_call x1, Pallas kernels: 5.99 us -> 6.97 us  [per_device(): pl.pallas_call(functools.partial(last_kernel, 1.0 / (rows * n), half, row...]
where the time goes in v4:
time: 37.2 us; the launch traced here: 37 us
  Pallas kernels  36.4 us (98%)
  between operations  0.64 us (2%)
    pallas_call x1, Pallas kernels, per_device(): pl.pallas_call(functools.partial(turning_kernel, n, n_pairs, half, rows),...  29.4 us
    pallas_call x1, Pallas kernels, per_device(): pl.pallas_call(functools.partial(last_kernel, 1.0 / (rows * n), half, row...  6.97 us

profile of v4, /device:TPU:0, one launch (start us, length us, event | category | flops | bytes accessed | tf_op | source)
XLA Modules:
  0.0 37.0 jit_solution(18354720691559760700)
XLA Ops:
  0.6 29.4 %shard_map.59 = (f32[16,256,128]{2,1,0:T(8,128)}, f32[8,8,128]{2,1,0:T(8,128)}) custom-call(f32[256,2048]{1,0:T(8,128)} %loads.1, f32[16,128]{1,0:T(8,128)} %bitcast.2, s32[2,2]{1,0:T(2,128)} %offsets.1, s32[2,8]{1,0:T(2,128)} %skips_in.1), custom_call_target="tpu_custom_call" | custom-call | flops 31457280 | bytes 4194304 | tf_op jit(solution)/shard_map/pallas_call | solution.py:432
  30.1 7.0 %shard_map.60 = (f32[256,2048]{1,0:T(8,128)}, f32[16,128]{1,0:T(8,128)}) custom-call(f32[16,256,128]{2,1,0:T(8,128)} %get-tuple-element.6.moved, f32[8,8,128]{2,1,0:T(8,128)} %get-tuple-element.7.coefs_in, s32[2,2]{1,0:T(2,128)} %offsets.1), custom_call_target="tpu_custom_call" | custom-call | flops 10485760 | bytes 4194304 | tf_op jit(solution)/shard_map/pallas_call | solution.py:468

commit v5 on v3

v5 whole, which is shorter than its diff:
```python
import functools
import jax
import jax.numpy as jnp
from jax import lax
from jax.experimental import pallas as pl
from jax.experimental.pallas import tpu as pltpu
from jax.sharding import PartitionSpec as P

BLOCK = 128
STEPS = 2
TILE = 8
CHUNK = 32
MESH = pl.DeviceIdType.MESH


def rolled(x, shift):
    return pltpu.roll(x, shift, 1)


def fold(x):
    return jnp.sum(x.reshape(x.shape[0] // TILE, TILE, BLOCK), axis=0)


def shifts_of(offsets, step):
    first, second = offsets[step, 0], offsets[step, 1]
    to_first = lax.rem(BLOCK - first, BLOCK)
    to_second = lax.rem(BLOCK - second, BLOCK)
    between = lax.rem(BLOCK + first - second, BLOCK)
    return to_first, to_second, between, second


def chunks(rows, body, carry):
    def step(at, carry):
        return body(pl.ds(pl.multiple_of(at * CHUNK, CHUNK), CHUNK), carry)

    return lax.fori_loop(0, rows // CHUNK, step, carry, unroll=True)


def products(upper, lower, shifts, turned, rows, partial):
    to_first, to_second, between, _ = shifts

    def body(spot, sums):
        u, l = upper[spot, :], lower[spot, :]
        lp, ud, ld = rolled(l, to_first), rolled(u, between), rolled(l, to_second)
        for at, x in enumerate((lp, ud, ld)):
            turned[at, spot, :] = x
        pairs = ((u, u), (l, l), (u, lp), (u, ud), (u, ld), (lp, ud), (lp, ld))
        return tuple(total + fold(a * b) for total, (a, b) in zip(sums, pairs))

    zero = jnp.zeros((TILE, BLOCK), jnp.float32)
    sums = chunks(rows, body, (zero,) * 7)
    for at, total in enumerate(sums):
        partial[pl.ds(at, 1), :] = jnp.sum(total, axis=0, keepdims=True)
    partial[pl.ds(7, 1), :] = jnp.zeros((1, BLOCK), jnp.float32)


def angle(a, b, g):
    half_gap = 0.5 * (b - a)
    sign = jnp.where(half_gap >= 0.0, 1.0, -1.0)
    denominator = jnp.maximum(
        jnp.abs(half_gap) + jnp.sqrt(half_gap * half_gap + g * g), 1e-06 * (a + b)
    )
    t = sign * g / denominator
    c = 1.0 / jnp.sqrt(1.0 + t * t)
    return c, t * c


def norms(a, b, g, c, s):
    cross = 2.0 * c * s * g
    return c * c * a - cross + s * s * b, s * s * a + cross + c * c * b


def turn(total, skip, shifts):
    to_first, _, between, back = shifts
    row = [jnp.broadcast_to(total[at : at + 1, :], (TILE, BLOCK)) for at in range(7)]
    a, b, g, u_ud, u_ld, l_ud, l_ld = row
    b = rolled(b, to_first)
    keep = jnp.full((TILE, BLOCK), skip, jnp.int32) == 0
    c, s = angle(a, b, g)
    c, s = jnp.where(keep, c, 1.0), jnp.where(keep, s, 0.0)
    a1, b1 = norms(a, b, g, c, s)
    cd, sd, bd = rolled(c, between), rolled(s, between), rolled(b1, between)
    g1 = c * (sd * u_ud + cd * u_ld) - s * (sd * l_ud + cd * l_ld)
    c2, s2 = angle(a1, bd, g1)
    c2, s2 = jnp.where(keep, c2, 1.0), jnp.where(keep, s2, 0.0)
    a2, b2 = norms(a1, bd, g1, c2, s2)
    place = lax.broadcasted_iota(jnp.int32, (TILE, BLOCK), 0)
    tile = rolled(b2, back)
    for at, value in enumerate((c, s, cd, sd, c2, s2, a2)):
        tile = jnp.where(place == at, value, tile)
    return tile


def rotate(upper, new_upper, new_lower, coefs, back, turned, rows):
    tile = coefs[...]
    c, s, cd, sd, c2, s2 = (tile[at : at + 1, :] for at in range(6))
    up = (c2 * c, -c2 * s, -s2 * sd, -s2 * cd)
    low = (s2 * c, -s2 * s, c2 * sd, c2 * cd)

    def body(spot, carry):
        parts = [upper[spot, :]] + [turned[at, spot, :] for at in range(3)]
        new_upper[spot, :] = sum(f * x for f, x in zip(up, parts))
        new_lower[spot, :] = rolled(sum(f * x for f, x in zip(low, parts)), back)
        return carry

    chunks(rows, body, 0)


def column_block(array, block):
    return array.at[:, pl.ds(pl.multiple_of(block * BLOCK, BLOCK), BLOCK)]


def turning_kernel(
    n, n_pairs, half, rows,
    data, offsets, skips,
    rotated, power,
    moved, partial, arrived, coefs, turned,
    give_sem, arrive_sem, spread_sem, coef_sem, pair_sem,
):
    me, position = lax.axis_index("rows"), lax.axis_index("pairs")
    copies = n // half
    own, group = me // copies, lax.rem(me, copies)
    not_first = (position + n_pairs - 1) // n_pairs
    is_last = (position + 1) // n_pairs

    barrier = pltpu.get_barrier_semaphore()

    @pl.loop(1, n)
    def _(by):
        pl.semaphore_signal(
            barrier, inc=1, device_id={"rows": lax.rem(me + by, n)}, device_id_type=MESH
        )

    @pl.when(position > 0)
    def _():
        pl.semaphore_signal(
            barrier, inc=1, device_id={"pairs": position - 1}, device_id_type=MESH
        )

    @pl.when(position < n_pairs - 1)
    def _():
        pl.semaphore_signal(
            barrier, inc=1, device_id={"pairs": position + 1}, device_id_type=MESH
        )

    def give(step, k):
        @pl.loop(0, copies)
        def _(at):
            to = k * copies + at

            @pl.when(to != me)
            def _():
                pltpu.make_async_remote_copy(
                    src_ref=partial.at[step, k],
                    dst_ref=arrived.at[step, me],
                    send_sem=give_sem.at[step],
                    recv_sem=arrive_sem.at[step],
                    device_id={"rows": to},
                    device_id_type=MESH,
                ).start()

            @pl.when(to == me)
            def _():
                arrived[step, me] = partial[step, k]

    def own_coefs(step, shifts):
        some = arrived.at[step, pl.ds(0, n - 1)]
        pltpu.make_async_copy(some, some, arrive_sem.at[step]).wait()
        total = jnp.sum(arrived[step], axis=0)
        coefs[step, own] = turn(total, skips[step, own], shifts)

        @pl.loop(1, half)
        def _(by):
            to = lax.rem(own + by, half) * copies + group
            pltpu.make_async_remote_copy(
                src_ref=coefs.at[step, own],
                dst_ref=coefs.at[step, own],
                send_sem=spread_sem.at[step],
                recv_sem=coef_sem.at[step, own],
                device_id={"rows": to},
                device_id_type=MESH,
            ).start()

    def wait_coefs(step, k):
        tile = coefs.at[step, k]

        @pl.when(k != own)
        def _():
            pltpu.make_async_copy(tile, tile, coef_sem.at[step, k]).wait()

    shifts, later = shifts_of(offsets, 0), shifts_of(offsets, 1)

    def first_products(k):
        products(
            column_block(data, k), column_block(data, half + k), shifts, turned.at[k],
            rows, partial.at[0, k],
        )

    early = half // 2

    @pl.loop(0, early)
    def _(k):
        first_products(k)

    pl.semaphore_wait(barrier, n - 1 + not_first + 1 - is_last)

    @pl.loop(0, early)
    def _(k):
        give(0, k)

    @pl.loop(early, half)
    def _(k):
        first_products(k)
        give(0, k)

    own_coefs(0, shifts)

    def first_turn(k, upper_to, lower_to):
        wait_coefs(0, k)
        rotate(
            column_block(data, k), moved.at[upper_to], moved.at[lower_to],
            coefs.at[0, k], shifts[3], turned.at[k], rows,
        )

    out_low, out_up = 2 * half, 2 * half + 1
    low_zero = (1 - not_first) + out_low * not_first
    up_last = (2 * half - 1) * is_last + out_up * (1 - is_last)
    up_copy = pltpu.make_async_remote_copy(
        src_ref=moved.at[out_up],
        dst_ref=moved.at[0],
        send_sem=pair_sem.at[0],
        recv_sem=pair_sem.at[1],
        device_id={"pairs": lax.rem(position + 1, n_pairs)},
        device_id_type=MESH,
    )
    low_copy = pltpu.make_async_remote_copy(
        src_ref=moved.at[out_low],
        dst_ref=moved.at[2 * half - 1],
        send_sem=pair_sem.at[2],
        recv_sem=pair_sem.at[3],
        device_id={"pairs": lax.rem(position + n_pairs - 1, n_pairs)},
        device_id_type=MESH,
    )

    first_turn(half - 1, up_last, 2 * half - 2)

    @pl.when(position < n_pairs - 1)
    def _():
        up_copy.start()

    first_turn(0, not_first, low_zero)

    @pl.when(position > 0)
    def _():
        low_copy.start()

    @pl.loop(1, half - 1)
    def _(k):
        first_turn(k, k + 1, half + k - 1)

    def second_products(k):
        products(
            moved.at[k], moved.at[half + k], later, turned.at[k], rows, partial.at[1, k]
        )
        give(1, k)

    @pl.loop(1, half - 1)
    def _(k):
        second_products(k)

    @pl.when(position > 0)
    def _():
        up_copy.wait_recv()

    second_products(0)

    @pl.when(position < n_pairs - 1)
    def _():
        low_copy.wait_recv()

    second_products(half - 1)
    own_coefs(1, later)

    @pl.loop(0, half)
    def _(k):
        wait_coefs(1, k)
        rotate(
            moved.at[k], column_block(rotated, k), column_block(rotated, half + k),
            coefs.at[1, k], later[3], turned.at[k], rows,
        )
        tile = coefs[1, k] * (1.0 / (rows * n))
        power[pl.ds(k, 1), :] = tile[6:7, :]
        power[pl.ds(half + k, 1), :] = tile[7:8, :]

    @pl.when(position > 0)
    def _():
        low_copy.wait_send()

    @pl.when(position < n_pairs - 1)
    def _():
        up_copy.wait_send()

    for step in range(STEPS):
        some = arrived.at[step, pl.ds(0, n - 1)]
        pltpu.make_async_copy(some, some, give_sem.at[step]).wait()
        rest = coefs.at[step, pl.ds(0, half - 1)]
        pltpu.make_async_copy(rest, rest, spread_sem.at[step]).wait()


def per_device(n, n_pairs, loads, col_weights, partner_offsets, skip_mask):
    rows, columns = loads.shape
    half = columns // (2 * BLOCK)
    tiles = (TILE, BLOCK)
    vmem = pl.BlockSpec(memory_space=pltpu.VMEM)
    smem = pl.BlockSpec(memory_space=pltpu.SMEM)
    dma = pltpu.SemaphoreType.DMA
    weighted = loads * col_weights[None, :]
    rotated, power = pl.pallas_call(
        functools.partial(turning_kernel, n, n_pairs, half, rows),
        out_shape=(
            jax.ShapeDtypeStruct(loads.shape, jnp.float32),
            jax.ShapeDtypeStruct((2 * half, BLOCK), jnp.float32),
        ),
        in_specs=[vmem, smem, smem],
        out_specs=(vmem, vmem),
        scratch_shapes=[
            pltpu.VMEM((2 * half + 2, rows, BLOCK), jnp.float32),
            pltpu.VMEM((STEPS, half) + tiles, jnp.float32),
            pltpu.VMEM((STEPS, n) + tiles, jnp.float32),
            pltpu.VMEM((STEPS, half) + tiles, jnp.float32),
            pltpu.VMEM((half, 3, rows, BLOCK), jnp.float32),
            dma((STEPS,)),
            dma((STEPS,)),
            dma((STEPS,)),
            dma((STEPS, half)),
            dma((4,)),
        ],
        compiler_params=pltpu.CompilerParams(
            collective_id=0, has_side_effects=True, vmem_limit_bytes=24 * 1024 * 1024
        ),
        cost_estimate=pl.CostEstimate(
            flops=60 * loads.size, bytes_accessed=8 * loads.size, transcendentals=0
        ),
    )(weighted, partner_offsets, skip_mask)
    return rotated, power.reshape(columns)


def solution(mesh):
    in_specs = (P("rows", "pairs"), P("pairs"), P(), P(None, "pairs"))
    out_specs = (P("rows", "pairs"), P("pairs"))
    return jax.shard_map(
        functools.partial(per_device, mesh.shape["rows"], mesh.shape["pairs"]),
        mesh=mesh, in_specs=in_specs, out_specs=out_specs, check_vma=False,
    )
```

time: 35.9 us -> 33.7 us (0.939)
  Pallas kernels: 35.1 us -> 29.1 us
  local copies, waits for them, and re-layouts: 0 us -> 1.93 us
  other arithmetic: 0 us -> 1.89 us
    pallas_call x1 -> x0, Pallas kernels: 5.99 us -> none  [per_device(): pl.pallas_call(functools.partial(last_kernel, 1.0 / (rows * n), half, row...]
    unnamed x0 -> x6, local copies, waits for them, and re-layouts: none -> 1.93 us
    mul x0 -> x1, other arithmetic: none -> 1.89 us  [per_device(): weighted = loads * col_weights[None, :]]
where the time goes in v5:
time: 33.7 us; the launch traced here: 33.6 us
  Pallas kernels  29.1 us (86%)
  local copies, waits for them, and re-layouts  1.93 us (6%)
  other arithmetic  1.89 us (6%)
  between operations  0.68 us (2%)
    pallas_call x1, Pallas kernels, per_device(): pl.pallas_call(functools.partial(turning_kernel, n, n_pairs, half, rows),...  29.1 us
    unnamed x6, local copies, waits for them, and re-layouts  1.93 us
    mul x1, other arithmetic, per_device(): weighted = loads * col_weights[None, :]  1.89 us

profile of v5, /device:TPU:0, one launch (start us, length us, event | category | flops | bytes accessed | tf_op | source)
XLA Modules:
  0.0 33.6 jit_solution(2196855751556575930)
XLA Ops:
  0.6 0.0 copy-start.1
  0.6 0.0 copy-start
  0.7 1.9 %broadcast_multiply_fusion.data = f32[256,2048]{1,0:T(8,128)S(1)} fusion(f32[256,2048]{1,0:T(8,128)} %param.4, f32[2048]{0:T(1024)} %param.5), kind=kLoop, calls=%fused_computation | loop fusion | flops 524288 | bytes 4202496 | tf_op jit(solution)/shard_map/mul | solution.py:317
  2.5 0.0 copy-done.1
  2.6 0.0 copy-done
  2.6 29.1 %shard_map.59 = (f32[256,2048]{1,0:T(8,128)S(1)}, f32[16,128]{1,0:T(8,128)S(1)}) custom-call(f32[256,2048]{1,0:T(8,128)S(1)} %broadcast_multiply_fusion.data, s32[2,2]{1,0:T(2,128)S(1)} %copy-done, s32[2,8]{1,0:T(2,128)S(1)} %copy-done.1), custom_call_target="tpu_custom_call" | custom-call | flops 31457280 | bytes 4194304 | tf_op jit(solution)/shard_map/pallas_call | solution.py:318
  31.7 1.3 %copy.8 = f32[256,2048]{1,0:T(8,128)} copy(f32[256,2048]{1,0:T(8,128)S(1)} %get-tuple-element.8) | data formatting | bytes 4194304
  33.0 0.6 %copy.9 = f32[2048]{0:T(1024)} copy(f32[2048]{0:T(1024)S(1)} %bitcast.1) | data formatting | bytes 16384
Async XLA Ops:
  0.6 1.9 %copy-start.1 = (s32[2,8]{1,0:T(2,128)S(1)}, s32[2,8]{1,0:T(2,128)}, u32[]{:S(2)}) copy-start(s32[2,8]{1,0:T(2,128)} %skips.1) | copy-start | bytes 196
  0.6 1.9 %copy-start = (s32[2,2]{1,0:T(2,128)S(1)}, s32[2,2]{1,0:T(2,128)}, u32[]{:S(2)}) copy-start(s32[2,2]{1,0:T(2,128)} %offsets.1) | copy-start | bytes 52

commit v6 on v5

--- a/solution.py
+++ b/solution.py
@@ -106,6 +106,10 @@
     chunks(rows, body, 0)
 
 
+def inner_size(half):
+    return 4 if half % 4 == 0 else 2
+
+
 def column_block(array, block):
     return array.at[:, pl.ds(pl.multiple_of(block * BLOCK, BLOCK), BLOCK)]
 
@@ -114,22 +118,31 @@
     n, n_pairs, half, rows,
     data, offsets, skips,
     rotated, power,
-    moved, partial, arrived, coefs, turned,
-    give_sem, arrive_sem, spread_sem, coef_sem, pair_sem,
+    moved, partial, near_parts, far_parts, coefs, turned,
+    give_sem, near_sem, pass_sem, far_sem, spread_sem, coef_sem, pair_sem,
 ):
     me, position = lax.axis_index("rows"), lax.axis_index("pairs")
-    copies = n // half
-    own, group = me // copies, lax.rem(me, copies)
+    near, share = inner_size(half), half // inner_size(half)
+    far = n // near
+    mine, line = lax.rem(me, near), me // near
     not_first = (position + n_pairs - 1) // n_pairs
     is_last = (position + 1) // n_pairs
 
     barrier = pltpu.get_barrier_semaphore()
 
-    @pl.loop(1, n)
-    def _(by):
-        pl.semaphore_signal(
-            barrier, inc=1, device_id={"rows": lax.rem(me + by, n)}, device_id_type=MESH
-        )
+    def near_device(by):
+        return line * near + lax.rem(mine + by, near)
+
+    def far_device(by):
+        return lax.rem(line + by, far) * near + mine
+
+    def greet(to):
+        pl.semaphore_signal(barrier, inc=1, device_id={"rows": to}, device_id_type=MESH)
+
+    for by in range(1, near):
+        greet(near_device(by))
+    for by in range(1, far):
+        greet(far_device(by))
 
     @pl.when(position > 0)
     def _():
@@ -143,50 +156,42 @@
             barrier, inc=1, device_id={"pairs": position + 1}, device_id_type=MESH
         )
 
-    def give(step, k):
-        @pl.loop(0, copies)
-        def _(at):
-            to = k * copies + at
-
-            @pl.when(to != me)
-            def _():
-                pltpu.make_async_remote_copy(
-                    src_ref=partial.at[step, k],
-                    dst_ref=arrived.at[step, me],
-                    send_sem=give_sem.at[step],
-                    recv_sem=arrive_sem.at[step],
-                    device_id={"rows": to},
-                    device_id_type=MESH,
-                ).start()
-
-            @pl.when(to == me)
-            def _():
-                arrived[step, me] = partial[step, k]
-
-    def own_coefs(step, shifts):
-        some = arrived.at[step, pl.ds(0, n - 1)]
-        pltpu.make_async_copy(some, some, arrive_sem.at[step]).wait()
-        total = jnp.sum(arrived[step], axis=0)
-        coefs[step, own] = turn(total, skips[step, own], shifts)
-
-        @pl.loop(1, half)
-        def _(by):
-            to = lax.rem(own + by, half) * copies + group
-            pltpu.make_async_remote_copy(
-                src_ref=coefs.at[step, own],
-                dst_ref=coefs.at[step, own],
-                send_sem=spread_sem.at[step],
-                recv_sem=coef_sem.at[step, own],
-                device_id={"rows": to},
-                device_id_type=MESH,
+    def pairs_of(at):
+        return pl.ds(at * share, share)
+
+    def send(source, target, to, sent, came):
+        return pltpu.make_async_remote_copy(
+            src_ref=source, dst_ref=target, send_sem=sent, recv_sem=came,
+            device_id={"rows": to}, device_id_type=MESH,
+        )
+
+    def wait_bytes(ref, sem):
+        pltpu.make_async_copy(ref, ref, sem).wait()
+
+    def give(step, at):
+        @pl.when(mine != at)
+        def _():
+            send(
+                partial.at[step, pairs_of(at)], near_parts.at[step, mine], line * near + at,
+                give_sem.at[step], near_sem.at[step],
             ).start()
 
-    def wait_coefs(step, k):
-        tile = coefs.at[step, k]
-
-        @pl.when(k != own)
-        def _():
-            pltpu.make_async_copy(tile, tile, coef_sem.at[step, k]).wait()
+    def all_coefs(step, shifts):
+        near_parts[step, mine] = partial[step, pairs_of(mine)]
+        wait_bytes(near_parts.at[step, pl.ds(0, near - 1)], near_sem.at[step])
+        far_parts[step, line] = jnp.sum(near_parts[step], axis=0)
+        for by in range(1, far):
+            own = far_parts.at[step, line]
+            send(own, own, far_device(by), pass_sem.at[step], far_sem.at[step]).start()
+        wait_bytes(far_parts.at[step, pl.ds(0, far - 1)], far_sem.at[step])
+        total = jnp.sum(far_parts[step], axis=0)
+        for at in range(share):
+            k = mine * share + at
+            coefs[step, k] = turn(total[at], skips[step, k], shifts)
+        for by in range(1, near):
+            own = coefs.at[step, pairs_of(mine)]
+            send(own, own, near_device(by), spread_sem.at[step], coef_sem.at[step]).start()
+        wait_bytes(coefs.at[step, pl.ds(0, (near - 1) * share)], coef_sem.at[step])
 
     shifts, later = shifts_of(offsets, 0), shifts_of(offsets, 1)
 
@@ -196,27 +201,24 @@
             rows, partial.at[0, k],
         )
 
-    early = half // 2
-
-    @pl.loop(0, early)
+    @pl.loop(0, share)
     def _(k):
         first_products(k)
 
-    pl.semaphore_wait(barrier, n - 1 + not_first + 1 - is_last)
-
-    @pl.loop(0, early)
-    def _(k):
-        give(0, k)
-
-    @pl.loop(early, half)
-    def _(k):
-        first_products(k)
-        give(0, k)
-
-    own_coefs(0, shifts)
+    pl.semaphore_wait(barrier, near + far - 2 + not_first + 1 - is_last)
+    give(0, 0)
+
+    @pl.loop(1, near)
+    def _(at):
+        @pl.loop(at * share, (at + 1) * share)
+        def _(k):
+            first_products(k)
+
+        give(0, at)
+
+    all_coefs(0, shifts)
 
     def first_turn(k, upper_to, lower_to):
-        wait_coefs(0, k)
         rotate(
             column_block(data, k), moved.at[upper_to], moved.at[lower_to],
             coefs.at[0, k], shifts[3], turned.at[k], rows,
@@ -262,28 +264,40 @@
         products(
             moved.at[k], moved.at[half + k], later, turned.at[k], rows, partial.at[1, k]
         )
-        give(1, k)
-
-    @pl.loop(1, half - 1)
+
+    @pl.loop(1, near - 1)
+    def _(at):
+        @pl.loop(at * share, (at + 1) * share)
+        def _(k):
+            second_products(k)
+
+        give(1, at)
+
+    @pl.loop(1, share)
     def _(k):
         second_products(k)
 
+    @pl.loop(half - share, half - 1)
+    def _(k):
+        second_products(k)
+
     @pl.when(position > 0)
     def _():
         up_copy.wait_recv()
 
     second_products(0)
+    give(1, 0)
 
     @pl.when(position < n_pairs - 1)
     def _():
         low_copy.wait_recv()
 
     second_products(half - 1)
-    own_coefs(1, later)
+    give(1, near - 1)
+    all_coefs(1, later)
 
     @pl.loop(0, half)
     def _(k):
-        wait_coefs(1, k)
         rotate(
             moved.at[k], column_block(rotated, k), column_block(rotated, half + k),
             coefs.at[1, k], later[3], turned.at[k], rows,
@@ -301,15 +315,15 @@
         up_copy.wait_send()
 
     for step in range(STEPS):
-        some = arrived.at[step, pl.ds(0, n - 1)]
-        pltpu.make_async_copy(some, some, give_sem.at[step]).wait()
-        rest = coefs.at[step, pl.ds(0, half - 1)]
-        pltpu.make_async_copy(rest, rest, spread_sem.at[step]).wait()
+        wait_bytes(near_parts.at[step, pl.ds(0, near - 1)], give_sem.at[step])
+        wait_bytes(far_parts.at[step, pl.ds(0, far - 1)], pass_sem.at[step])
+        wait_bytes(coefs.at[step, pl.ds(0, (near - 1) * share)], spread_sem.at[step])
 
 
 def per_device(n, n_pairs, loads, col_weights, partner_offsets, skip_mask):
     rows, columns = loads.shape
     half = columns // (2 * BLOCK)
+    near = inner_size(half)
     tiles = (TILE, BLOCK)
     vmem = pl.BlockSpec(memory_space=pltpu.VMEM)
     smem = pl.BlockSpec(memory_space=pltpu.SMEM)
@@ -326,13 +340,16 @@
         scratch_shapes=[
             pltpu.VMEM((2 * half + 2, rows, BLOCK), jnp.float32),
             pltpu.VMEM((STEPS, half) + tiles, jnp.float32),
-            pltpu.VMEM((STEPS, n) + tiles, jnp.float32),
+            pltpu.VMEM((STEPS, near, half // near) + tiles, jnp.float32),
+            pltpu.VMEM((STEPS, n // near, half // near) + tiles, jnp.float32),
             pltpu.VMEM((STEPS, half) + tiles, jnp.float32),
             pltpu.VMEM((half, 3, rows, BLOCK), jnp.float32),
             dma((STEPS,)),
             dma((STEPS,)),
             dma((STEPS,)),
-            dma((STEPS, half)),
+            dma((STEPS,)),
+            dma((STEPS,)),
+            dma((STEPS,)),
             dma((4,)),
         ],
         compiler_params=pltpu.CompilerParams(

time: 33.7 us -> 34.6 us (1.027)
  Pallas kernels: 29.1 us -> 30 us
    pallas_call x1, Pallas kernels: 29.1 us -> 30 us  [per_device(): pl.pallas_call(functools.partial(turning_kernel, n, n_pairs, half, rows),...]
where the time goes in v6:
time: 34.6 us; the launch traced here: 34.5 us
  Pallas kernels  30 us (87%)
  local copies, waits for them, and re-layouts  1.93 us (6%)
  other arithmetic  1.89 us (5%)
  between operations  0.68 us (2%)
    pallas_call x1, Pallas kernels, per_device(): pl.pallas_call(functools.partial(turning_kernel, n, n_pairs, half, rows),...  30 us
    unnamed x6, local copies, waits for them, and re-layouts  1.93 us
    mul x1, other arithmetic, per_device(): weighted = loads * col_weights[None, :]  1.89 us

profile of v6, /device:TPU:0, one launch (start us, length us, event | category | flops | bytes accessed | tf_op | source)
XLA Modules:
  0.0 34.5 jit_solution(2396386345283112829)
XLA Ops:
  0.6 0.0 copy-start.1
  0.6 0.0 copy-start
  0.7 1.9 %broadcast_multiply_fusion.data = f32[256,2048]{1,0:T(8,128)S(1)} fusion(f32[256,2048]{1,0:T(8,128)} %param.4, f32[2048]{0:T(1024)} %param.5), kind=kLoop, calls=%fused_computation | loop fusion | flops 524288 | bytes 4202496 | tf_op jit(solution)/shard_map/mul | solution.py:331
  2.5 0.0 copy-done.1
  2.6 0.0 copy-done
  2.6 30.0 %shard_map.59 = (f32[256,2048]{1,0:T(8,128)S(1)}, f32[16,128]{1,0:T(8,128)S(1)}) custom-call(f32[256,2048]{1,0:T(8,128)S(1)} %broadcast_multiply_fusion.data, s32[2,2]{1,0:T(2,128)S(1)} %copy-done, s32[2,8]{1,0:T(2,128)S(1)} %copy-done.1), custom_call_target="tpu_custom_call" | custom-call | flops 31457280 | bytes 4194304 | tf_op jit(solution)/shard_map/pallas_call | solution.py:332
  32.5 1.3 %copy.8 = f32[256,2048]{1,0:T(8,128)} copy(f32[256,2048]{1,0:T(8,128)S(1)} %get-tuple-element.8) | data formatting | bytes 4194304
  33.9 0.6 %copy.9 = f32[2048]{0:T(1024)} copy(f32[2048]{0:T(1024)S(1)} %bitcast.1) | data formatting | bytes 16384
Async XLA Ops:
  0.6 1.9 %copy-start.1 = (s32[2,8]{1,0:T(2,128)S(1)}, s32[2,8]{1,0:T(2,128)}, u32[]{:S(2)}) copy-start(s32[2,8]{1,0:T(2,128)} %skips.1) | copy-start | bytes 196
  0.6 1.9 %copy-start = (s32[2,2]{1,0:T(2,128)S(1)}, s32[2,2]{1,0:T(2,128)}, u32[]{:S(2)}) copy-start(s32[2,2]{1,0:T(2,128)} %offsets.1) | copy-start | bytes 52

commit v7 on v5

--- a/solution.py
+++ b/solution.py
@@ -91,16 +91,43 @@
     return tile
 
 
-def rotate(upper, new_upper, new_lower, coefs, back, turned, rows):
+def factors(coefs):
     tile = coefs[...]
-    c, s, cd, sd, c2, s2 = (tile[at : at + 1, :] for at in range(6))
+    c, s, cd, sd, c2, s2 = (
+        jnp.broadcast_to(tile[at : at + 1, :], (TILE, BLOCK)) for at in range(6)
+    )
     up = (c2 * c, -c2 * s, -s2 * sd, -s2 * cd)
     low = (s2 * c, -s2 * s, c2 * sd, c2 * cd)
+    return up, low
+
+
+def mix(weights, parts):
+    shape = (CHUNK // TILE, TILE, BLOCK)
+    total = sum(w[None] * x.reshape(shape) for w, x in zip(weights, parts))
+    return total.reshape(CHUNK, BLOCK)
+
+
+def rotate(upper, new_upper, new_lower, coefs, back, turned, rows):
+    up, low = factors(coefs)
 
     def body(spot, carry):
         parts = [upper[spot, :]] + [turned[at, spot, :] for at in range(3)]
-        new_upper[spot, :] = sum(f * x for f, x in zip(up, parts))
-        new_lower[spot, :] = rolled(sum(f * x for f, x in zip(low, parts)), back)
+        new_upper[spot, :] = mix(up, parts)
+        new_lower[spot, :] = rolled(mix(low, parts), back)
+        return carry
+
+    chunks(rows, body, 0)
+
+
+def rotate_one(pair, new, coefs, shifts, rows, which):
+    weights = factors(coefs)[which]
+    to_first, to_second, between, back = shifts
+
+    def body(spot, carry):
+        u, l = pair[0, spot, :], pair[1, spot, :]
+        parts = (u, rolled(l, to_first), rolled(u, between), rolled(l, to_second))
+        x = mix(weights, parts)
+        new[spot, :] = rolled(x, back) if which else x
         return carry
 
     chunks(rows, body, 0)
@@ -114,8 +141,8 @@
     n, n_pairs, half, rows,
     data, offsets, skips,
     rotated, power,
-    moved, partial, arrived, coefs, turned,
-    give_sem, arrive_sem, spread_sem, coef_sem, pair_sem,
+    moved, partial, arrived, coefs, turned, guests, guest_coefs,
+    give_sem, arrive_sem, spread_sem, coef_sem, guest_sem, guest_coef_sem,
 ):
     me, position = lax.axis_index("rows"), lax.axis_index("pairs")
     copies = n // half
@@ -131,17 +158,23 @@
             barrier, inc=1, device_id={"rows": lax.rem(me + by, n)}, device_id_type=MESH
         )
 
+    def greet_pairs(to):
+        pl.semaphore_signal(barrier, inc=1, device_id={"pairs": to}, device_id_type=MESH)
+
+        @pl.loop(0, half)
+        def _(at):
+            pl.semaphore_signal(
+                barrier, inc=1,
+                device_id={"rows": at * copies + group, "pairs": to}, device_id_type=MESH,
+            )
+
     @pl.when(position > 0)
     def _():
-        pl.semaphore_signal(
-            barrier, inc=1, device_id={"pairs": position - 1}, device_id_type=MESH
-        )
+        greet_pairs(position - 1)
 
     @pl.when(position < n_pairs - 1)
     def _():
-        pl.semaphore_signal(
-            barrier, inc=1, device_id={"pairs": position + 1}, device_id_type=MESH
-        )
+        greet_pairs(position + 1)
 
     def give(step, k):
         @pl.loop(0, copies)
@@ -181,6 +214,39 @@
                 device_id_type=MESH,
             ).start()
 
+    has_next, has_last = position < n_pairs - 1, position > 0
+    after, before = lax.rem(position + 1, n_pairs), lax.rem(position + n_pairs - 1, n_pairs)
+
+    def lend(k, side, to):
+        for at, block in enumerate((k, half + k)):
+            pltpu.make_async_remote_copy(
+                src_ref=column_block(data, block),
+                dst_ref=guests.at[side, at],
+                send_sem=guest_sem.at[side, 0],
+                recv_sem=guest_sem.at[side, 1],
+                device_id={"pairs": to},
+                device_id_type=MESH,
+            ).start()
+
+    def lend_coefs(k, side, to):
+        @pl.loop(0, half)
+        def _(at):
+            pltpu.make_async_remote_copy(
+                src_ref=coefs.at[0, k],
+                dst_ref=guest_coefs.at[side],
+                send_sem=guest_coef_sem.at[side, 0],
+                recv_sem=guest_coef_sem.at[side, 1],
+                device_id={"rows": at * copies + group, "pairs": to},
+                device_id_type=MESH,
+            ).start()
+
+    def wait_bytes(ref, sem):
+        pltpu.make_async_copy(ref, ref, sem).wait()
+
+    def wait_guest(side):
+        wait_bytes(guests.at[side], guest_sem.at[side, 1])
+        wait_bytes(guest_coefs.at[side], guest_coef_sem.at[side, 1])
+
     def wait_coefs(step, k):
         tile = coefs.at[step, k]
 
@@ -202,7 +268,16 @@
     def _(k):
         first_products(k)
 
-    pl.semaphore_wait(barrier, n - 1 + not_first + 1 - is_last)
+    pl.semaphore_wait(barrier, n - 1 + (1 + half) * (not_first + 1 - is_last))
+
+    @pl.when(has_next)
+    def _():
+        lend(half - 1, 0, after)
+
+    @pl.when(has_last)
+    def _():
+        lend(0, 1, before)
+
 
     @pl.loop(0, early)
     def _(k):
@@ -214,6 +289,14 @@
         give(0, k)
 
     own_coefs(0, shifts)
+
+    @pl.when(has_next & (own == half - 1))
+    def _():
+        lend_coefs(half - 1, 0, after)
+
+    @pl.when(has_last & (own == 0))
+    def _():
+        lend_coefs(0, 1, before)
 
     def first_turn(k, upper_to, lower_to):
         wait_coefs(0, k)
@@ -225,34 +308,8 @@
     out_low, out_up = 2 * half, 2 * half + 1
     low_zero = (1 - not_first) + out_low * not_first
     up_last = (2 * half - 1) * is_last + out_up * (1 - is_last)
-    up_copy = pltpu.make_async_remote_copy(
-        src_ref=moved.at[out_up],
-        dst_ref=moved.at[0],
-        send_sem=pair_sem.at[0],
-        recv_sem=pair_sem.at[1],
-        device_id={"pairs": lax.rem(position + 1, n_pairs)},
-        device_id_type=MESH,
-    )
-    low_copy = pltpu.make_async_remote_copy(
-        src_ref=moved.at[out_low],
-        dst_ref=moved.at[2 * half - 1],
-        send_sem=pair_sem.at[2],
-        recv_sem=pair_sem.at[3],
-        device_id={"pairs": lax.rem(position + n_pairs - 1, n_pairs)},
-        device_id_type=MESH,
-    )
-
     first_turn(half - 1, up_last, 2 * half - 2)
-
-    @pl.when(position < n_pairs - 1)
-    def _():
-        up_copy.start()
-
     first_turn(0, not_first, low_zero)
-
-    @pl.when(position > 0)
-    def _():
-        low_copy.start()
 
     @pl.loop(1, half - 1)
     def _(k):
@@ -270,13 +327,15 @@
 
     @pl.when(position > 0)
     def _():
-        up_copy.wait_recv()
+        wait_guest(0)
+        rotate_one(guests.at[0], moved.at[0], guest_coefs.at[0], shifts, rows, 0)
 
     second_products(0)
 
     @pl.when(position < n_pairs - 1)
     def _():
-        low_copy.wait_recv()
+        wait_guest(1)
+        rotate_one(guests.at[1], moved.at[2 * half - 1], guest_coefs.at[1], shifts, rows, 1)
 
     second_products(half - 1)
     own_coefs(1, later)
@@ -292,13 +351,15 @@
         power[pl.ds(k, 1), :] = tile[6:7, :]
         power[pl.ds(half + k, 1), :] = tile[7:8, :]
 
-    @pl.when(position > 0)
-    def _():
-        low_copy.wait_send()
-
-    @pl.when(position < n_pairs - 1)
-    def _():
-        up_copy.wait_send()
+    for side, lent, lender in ((0, has_next, half - 1), (1, has_last, 0)):
+
+        @pl.when(lent)
+        def _():
+            wait_bytes(guests.at[side], guest_sem.at[side, 0])
+
+        @pl.when(lent & (own == lender))
+        def _():
+            wait_bytes(coefs.at[0], guest_coef_sem.at[side, 0])
 
     for step in range(STEPS):
         some = arrived.at[step, pl.ds(0, n - 1)]
@@ -329,11 +390,14 @@
             pltpu.VMEM((STEPS, n) + tiles, jnp.float32),
             pltpu.VMEM((STEPS, half) + tiles, jnp.float32),
             pltpu.VMEM((half, 3, rows, BLOCK), jnp.float32),
+            pltpu.VMEM((2, 2, rows, BLOCK), jnp.float32),
+            pltpu.VMEM((2,) + tiles, jnp.float32),
             dma((STEPS,)),
             dma((STEPS,)),
             dma((STEPS,)),
             dma((STEPS, half)),
-            dma((4,)),
+            dma((2, 2)),
+            dma((2, 2)),
         ],
         compiler_params=pltpu.CompilerParams(
             collective_id=0, has_side_effects=True, vmem_limit_bytes=24 * 1024 * 1024

time: 33.7 us -> 33.1 us (0.982)
  Pallas kernels: 29.1 us -> 28.4 us
    pallas_call x1, Pallas kernels: 29.1 us -> 28.4 us  [per_device(): pl.pallas_call(functools.partial(turning_kernel, n, n_pairs, half, rows),...]
where the time goes in v7:
time: 33.1 us; the launch traced here: 32.9 us
  Pallas kernels  28.4 us (86%)
  local copies, waits for them, and re-layouts  1.93 us (6%)
  other arithmetic  1.89 us (6%)
  between operations  0.68 us (2%)
    pallas_call x1, Pallas kernels, per_device(): pl.pallas_call(functools.partial(turning_kernel, n, n_pairs, half, rows),...  28.4 us
    unnamed x6, local copies, waits for them, and re-layouts  1.93 us
    mul x1, other arithmetic, per_device(): weighted = loads * col_weights[None, :]  1.89 us

profile of v7, /device:TPU:0, one launch (start us, length us, event | category | flops | bytes accessed | tf_op | source)
XLA Modules:
  0.0 32.9 jit_solution(2388106470920877741)
XLA Ops:
  0.6 0.0 copy-start.1
  0.6 0.0 copy-start
  0.7 1.9 %broadcast_multiply_fusion.data = f32[256,2048]{1,0:T(8,128)S(1)} fusion(f32[256,2048]{1,0:T(8,128)} %param.4, f32[2048]{0:T(1024)} %param.5), kind=kLoop, calls=%fused_computation | loop fusion | flops 524288 | bytes 4202496 | tf_op jit(solution)/shard_map/mul | solution.py:378
  2.5 0.0 copy-done.1
  2.6 0.0 copy-done
  2.6 28.4 %shard_map.59 = (f32[256,2048]{1,0:T(8,128)S(1)}, f32[16,128]{1,0:T(8,128)S(1)}) custom-call(f32[256,2048]{1,0:T(8,128)S(1)} %broadcast_multiply_fusion.data, s32[2,2]{1,0:T(2,128)S(1)} %copy-done, s32[2,8]{1,0:T(2,128)S(1)} %copy-done.1), custom_call_target="tpu_custom_call" | custom-call | flops 31457280 | bytes 4194304 | tf_op jit(solution)/shard_map/pallas_call | solution.py:379
  31.0 1.3 %copy.8 = f32[256,2048]{1,0:T(8,128)} copy(f32[256,2048]{1,0:T(8,128)S(1)} %get-tuple-element.8) | data formatting | bytes 4194304
  32.3 0.6 %copy.9 = f32[2048]{0:T(1024)} copy(f32[2048]{0:T(1024)S(1)} %bitcast.1) | data formatting | bytes 16384
Async XLA Ops:
  0.6 1.9 %copy-start.1 = (s32[2,8]{1,0:T(2,128)S(1)}, s32[2,8]{1,0:T(2,128)}, u32[]{:S(2)}) copy-start(s32[2,8]{1,0:T(2,128)} %skips.1) | copy-start | bytes 196
  0.6 1.9 %copy-start = (s32[2,2]{1,0:T(2,128)S(1)}, s32[2,2]{1,0:T(2,128)}, u32[]{:S(2)}) copy-start(s32[2,2]{1,0:T(2,128)} %offsets.1) | copy-start | bytes 52

commit v8 on v7

--- a/solution.py
+++ b/solution.py
@@ -10,6 +10,7 @@
 STEPS = 2
 TILE = 8
 CHUNK = 32
+DEPTH = 2
 MESH = pl.DeviceIdType.MESH
 
 
@@ -29,29 +30,43 @@
     return to_first, to_second, between, second
 
 
-def chunks(rows, body, carry):
-    def step(at, carry):
-        return body(pl.ds(pl.multiple_of(at * CHUNK, CHUNK), CHUNK), carry)
-
-    return lax.fori_loop(0, rows // CHUNK, step, carry, unroll=True)
-
-
-def products(upper, lower, shifts, turned, rows, partial):
+def spots(rows):
+    return [pl.ds(at * CHUNK, CHUNK) for at in range(rows // CHUNK)]
+
+
+class Later:
+    def __init__(self):
+        self.waiting = []
+
+    def add(self, stores):
+        self.waiting.append(stores)
+        if len(self.waiting) > DEPTH:
+            self.write(self.waiting.pop(0))
+
+    def write(self, stores):
+        for ref, index, value in stores:
+            ref[index] = value
+
+    def end(self):
+        for stores in self.waiting:
+            self.write(stores)
+
+
+def products(pairs, shifts, rows):
     to_first, to_second, between, _ = shifts
-
-    def body(spot, sums):
-        u, l = upper[spot, :], lower[spot, :]
-        lp, ud, ld = rolled(l, to_first), rolled(u, between), rolled(l, to_second)
-        for at, x in enumerate((lp, ud, ld)):
-            turned[at, spot, :] = x
-        pairs = ((u, u), (l, l), (u, lp), (u, ud), (u, ld), (lp, ud), (lp, ld))
-        return tuple(total + fold(a * b) for total, (a, b) in zip(sums, pairs))
-
-    zero = jnp.zeros((TILE, BLOCK), jnp.float32)
-    sums = chunks(rows, body, (zero,) * 7)
-    for at, total in enumerate(sums):
-        partial[pl.ds(at, 1), :] = jnp.sum(total, axis=0, keepdims=True)
-    partial[pl.ds(7, 1), :] = jnp.zeros((1, BLOCK), jnp.float32)
+    later = Later()
+    for upper, lower, turned, partial in pairs:
+        sums = [jnp.zeros((TILE, BLOCK), jnp.float32)] * 7
+        for spot in spots(rows):
+            u, l = upper[spot, :], lower[spot, :]
+            lp, ud, ld = rolled(l, to_first), rolled(u, between), rolled(l, to_second)
+            factor_pairs = ((u, u), (l, l), (u, lp), (u, ud), (u, ld), (lp, ud), (lp, ld))
+            sums = [total + fold(a * b) for total, (a, b) in zip(sums, factor_pairs)]
+            later.add([(turned, (at, spot), x) for at, x in enumerate((lp, ud, ld))])
+        ends = [jnp.sum(total, axis=0, keepdims=True) for total in sums]
+        ends.append(jnp.zeros((1, BLOCK), jnp.float32))
+        later.add([(partial, pl.ds(at, 1), x) for at, x in enumerate(ends)])
+    later.end()
 
 
 def angle(a, b, g):
@@ -107,30 +122,27 @@
     return total.reshape(CHUNK, BLOCK)
 
 
-def rotate(upper, new_upper, new_lower, coefs, back, turned, rows):
-    up, low = factors(coefs)
-
-    def body(spot, carry):
-        parts = [upper[spot, :]] + [turned[at, spot, :] for at in range(3)]
-        new_upper[spot, :] = mix(up, parts)
-        new_lower[spot, :] = rolled(mix(low, parts), back)
-        return carry
-
-    chunks(rows, body, 0)
+def rotate(pairs, back, rows):
+    later = Later()
+    weights = [factors(pair[3]) for pair in pairs]
+    for (upper, new_upper, new_lower, _, turned), (up, low) in zip(pairs, weights):
+        for spot in spots(rows):
+            parts = [upper[spot, :]] + [turned[at, spot, :] for at in range(3)]
+            low_part = rolled(mix(low, parts), back)
+            later.add([(new_upper, spot, mix(up, parts)), (new_lower, spot, low_part)])
+    later.end()
 
 
 def rotate_one(pair, new, coefs, shifts, rows, which):
     weights = factors(coefs)[which]
     to_first, to_second, between, back = shifts
-
-    def body(spot, carry):
+    later = Later()
+    for spot in spots(rows):
         u, l = pair[0, spot, :], pair[1, spot, :]
         parts = (u, rolled(l, to_first), rolled(u, between), rolled(l, to_second))
         x = mix(weights, parts)
-        new[spot, :] = rolled(x, back) if which else x
-        return carry
-
-    chunks(rows, body, 0)
+        later.add([(new, spot, rolled(x, back) if which else x)])
+    later.end()
 
 
 def column_block(array, block):
@@ -256,17 +268,18 @@
 
     shifts, later = shifts_of(offsets, 0), shifts_of(offsets, 1)
 
-    def first_products(k):
-        products(
-            column_block(data, k), column_block(data, half + k), shifts, turned.at[k],
-            rows, partial.at[0, k],
-        )
-
-    early = half // 2
+    def first_pair(k):
+        upper, lower = column_block(data, k), column_block(data, half + k)
+        return upper, lower, turned.at[k], partial.at[0, k]
+
+    def second_pair(k):
+        return moved.at[k], moved.at[half + k], turned.at[k], partial.at[1, k]
+
+    early = half // 4
 
     @pl.loop(0, early)
-    def _(k):
-        first_products(k)
+    def _(at):
+        products([first_pair(2 * at), first_pair(2 * at + 1)], shifts, rows)
 
     pl.semaphore_wait(barrier, n - 1 + (1 + half) * (not_first + 1 - is_last))
 
@@ -279,14 +292,15 @@
         lend(0, 1, before)
 
 
-    @pl.loop(0, early)
+    @pl.loop(0, 2 * early)
     def _(k):
         give(0, k)
 
-    @pl.loop(early, half)
-    def _(k):
-        first_products(k)
-        give(0, k)
+    @pl.loop(early, half // 2)
+    def _(at):
+        products([first_pair(2 * at), first_pair(2 * at + 1)], shifts, rows)
+        give(0, 2 * at)
+        give(0, 2 * at + 1)
 
     own_coefs(0, shifts)
 
@@ -299,57 +313,60 @@
         lend_coefs(0, 1, before)
 
     def first_turn(k, upper_to, lower_to):
-        wait_coefs(0, k)
-        rotate(
-            column_block(data, k), moved.at[upper_to], moved.at[lower_to],
-            coefs.at[0, k], shifts[3], turned.at[k], rows,
-        )
+        upper = column_block(data, k)
+        return upper, moved.at[upper_to], moved.at[lower_to], coefs.at[0, k], turned.at[k]
+
+    def last_turn(k):
+        upper, lower = column_block(rotated, k), column_block(rotated, half + k)
+        return moved.at[k], upper, lower, coefs.at[1, k], turned.at[k]
 
     out_low, out_up = 2 * half, 2 * half + 1
     low_zero = (1 - not_first) + out_low * not_first
     up_last = (2 * half - 1) * is_last + out_up * (1 - is_last)
-    first_turn(half - 1, up_last, 2 * half - 2)
-    first_turn(0, not_first, low_zero)
-
-    @pl.loop(1, half - 1)
-    def _(k):
-        first_turn(k, k + 1, half + k - 1)
-
-    def second_products(k):
-        products(
-            moved.at[k], moved.at[half + k], later, turned.at[k], rows, partial.at[1, k]
-        )
-        give(1, k)
-
-    @pl.loop(1, half - 1)
-    def _(k):
-        second_products(k)
+    wait_coefs(0, half - 1)
+    wait_coefs(0, 0)
+    ends = [first_turn(half - 1, up_last, 2 * half - 2), first_turn(0, not_first, low_zero)]
+    rotate(ends, shifts[3], rows)
+
+    @pl.loop(0, half // 2 - 1)
+    def _(at):
+        inner = (2 * at + 1, 2 * at + 2)
+        for k in inner:
+            wait_coefs(0, k)
+        rotate([first_turn(k, k + 1, half + k - 1) for k in inner], shifts[3], rows)
+
+    @pl.loop(0, half // 2 - 1)
+    def _(at):
+        inner = (2 * at + 1, 2 * at + 2)
+        products([second_pair(k) for k in inner], later, rows)
+        for k in inner:
+            give(1, k)
 
     @pl.when(position > 0)
     def _():
         wait_guest(0)
         rotate_one(guests.at[0], moved.at[0], guest_coefs.at[0], shifts, rows, 0)
 
-    second_products(0)
-
     @pl.when(position < n_pairs - 1)
     def _():
         wait_guest(1)
         rotate_one(guests.at[1], moved.at[2 * half - 1], guest_coefs.at[1], shifts, rows, 1)
 
-    second_products(half - 1)
+    products([second_pair(0), second_pair(half - 1)], later, rows)
+    give(1, 0)
+    give(1, half - 1)
     own_coefs(1, later)
 
-    @pl.loop(0, half)
-    def _(k):
-        wait_coefs(1, k)
-        rotate(
-            moved.at[k], column_block(rotated, k), column_block(rotated, half + k),
-            coefs.at[1, k], later[3], turned.at[k], rows,
-        )
-        tile = coefs[1, k] * (1.0 / (rows * n))
-        power[pl.ds(k, 1), :] = tile[6:7, :]
-        power[pl.ds(half + k, 1), :] = tile[7:8, :]
+    @pl.loop(0, half // 2)
+    def _(at):
+        two = (2 * at, 2 * at + 1)
+        for k in two:
+            wait_coefs(1, k)
+        rotate([last_turn(k) for k in two], later[3], rows)
+        for k in two:
+            tile = coefs[1, k] * (1.0 / (rows * n))
+            power[pl.ds(k, 1), :] = tile[6:7, :]
+            power[pl.ds(half + k, 1), :] = tile[7:8, :]
 
     for side, lent, lender in ((0, has_next, half - 1), (1, has_last, 0)):
 

time: 33.1 us -> 32.5 us (0.982)
  Pallas kernels: 28.4 us -> 27.8 us
    pallas_call x1, Pallas kernels: 28.4 us -> 27.8 us  [per_device(): pl.pallas_call(functools.partial(turning_kernel, n, n_pairs, half, rows),...]
where the time goes in v8:
time: 32.5 us; the launch traced here: 32.3 us
  Pallas kernels  27.8 us (86%)
  local copies, waits for them, and re-layouts  1.93 us (6%)
  other arithmetic  1.89 us (6%)
  between operations  0.68 us (2%)
    pallas_call x1, Pallas kernels, per_device(): pl.pallas_call(functools.partial(turning_kernel, n, n_pairs, half, rows),...  27.8 us
    unnamed x6, local copies, waits for them, and re-layouts  1.93 us
    mul x1, other arithmetic, per_device(): weighted = loads * col_weights[None, :]  1.89 us

profile of v8, /device:TPU:0, one launch (start us, length us, event | category | flops | bytes accessed | tf_op | source)
XLA Modules:
  0.0 32.3 jit_solution(17094265290294998288)
XLA Ops:
  0.6 0.0 copy-start.1
  0.6 0.0 copy-start
  0.7 1.9 %broadcast_multiply_fusion.data = f32[256,2048]{1,0:T(8,128)S(1)} fusion(f32[256,2048]{1,0:T(8,128)} %param.4, f32[2048]{0:T(1024)} %param.5), kind=kLoop, calls=%fused_computation | loop fusion | flops 524288 | bytes 4202496 | tf_op jit(solution)/shard_map/mul | solution.py:395
  2.5 0.0 copy-done.1
  2.6 0.0 copy-done
  2.6 27.8 %shard_map.59 = (f32[256,2048]{1,0:T(8,128)S(1)}, f32[16,128]{1,0:T(8,128)S(1)}) custom-call(f32[256,2048]{1,0:T(8,128)S(1)} %broadcast_multiply_fusion.data, s32[2,2]{1,0:T(2,128)S(1)} %copy-done, s32[2,8]{1,0:T(2,128)S(1)} %copy-done.1), custom_call_target="tpu_custom_call" | custom-call | flops 31457280 | bytes 4194304 | tf_op jit(solution)/shard_map/pallas_call | solution.py:396
  30.4 1.3 %copy.8 = f32[256,2048]{1,0:T(8,128)} copy(f32[256,2048]{1,0:T(8,128)S(1)} %get-tuple-element.8) | data formatting | bytes 4194304
  31.7 0.6 %copy.9 = f32[2048]{0:T(1024)} copy(f32[2048]{0:T(1024)S(1)} %bitcast.1) | data formatting | bytes 16384
Async XLA Ops:
  0.6 1.9 %copy-start.1 = (s32[2,8]{1,0:T(2,128)S(1)}, s32[2,8]{1,0:T(2,128)}, u32[]{:S(2)}) copy-start(s32[2,8]{1,0:T(2,128)} %skips.1) | copy-start | bytes 196
  0.6 1.9 %copy-start = (s32[2,2]{1,0:T(2,128)S(1)}, s32[2,2]{1,0:T(2,128)}, u32[]{:S(2)}) copy-start(s32[2,2]{1,0:T(2,128)} %offsets.1) | copy-start | bytes 52

commit v9 on v8

--- a/solution.py
+++ b/solution.py
@@ -323,24 +323,30 @@
     out_low, out_up = 2 * half, 2 * half + 1
     low_zero = (1 - not_first) + out_low * not_first
     up_last = (2 * half - 1) * is_last + out_up * (1 - is_last)
+    def turn_inner(k):
+        for each in (k, k + 1):
+            wait_coefs(0, each)
+        rotate([first_turn(each, each + 1, half + each - 1) for each in (k, k + 1)], shifts[3], rows)
+
+    def multiply(ks):
+        products([second_pair(k) for k in ks], later, rows)
+        for k in ks:
+            give(1, k)
+
+    if half > 2:
+        turn_inner(1)
+
+    @pl.loop(1, half // 2 - 1)
+    def _(at):
+        turn_inner(2 * at + 1)
+        multiply((2 * at, 2 * at + 1))
+
+    wait_coefs(0, 0)
     wait_coefs(0, half - 1)
-    wait_coefs(0, 0)
     ends = [first_turn(half - 1, up_last, 2 * half - 2), first_turn(0, not_first, low_zero)]
     rotate(ends, shifts[3], rows)
-
-    @pl.loop(0, half // 2 - 1)
-    def _(at):
-        inner = (2 * at + 1, 2 * at + 2)
-        for k in inner:
-            wait_coefs(0, k)
-        rotate([first_turn(k, k + 1, half + k - 1) for k in inner], shifts[3], rows)
-
-    @pl.loop(0, half // 2 - 1)
-    def _(at):
-        inner = (2 * at + 1, 2 * at + 2)
-        products([second_pair(k) for k in inner], later, rows)
-        for k in inner:
-            give(1, k)
+    if half > 2:
+        multiply((1, half - 2))
 
     @pl.when(position > 0)
     def _():
@@ -352,21 +358,25 @@
         wait_guest(1)
         rotate_one(guests.at[1], moved.at[2 * half - 1], guest_coefs.at[1], shifts, rows, 1)
 
-    products([second_pair(0), second_pair(half - 1)], later, rows)
-    give(1, 0)
-    give(1, half - 1)
+    multiply((0, half - 1))
     own_coefs(1, later)
 
-    @pl.loop(0, half // 2)
-    def _(at):
-        two = (2 * at, 2 * at + 1)
-        for k in two:
+    def turn_last(ks):
+        for k in ks:
             wait_coefs(1, k)
-        rotate([last_turn(k) for k in two], later[3], rows)
-        for k in two:
+        rotate([last_turn(k) for k in ks], later[3], rows)
+        for k in ks:
             tile = coefs[1, k] * (1.0 / (rows * n))
             power[pl.ds(k, 1), :] = tile[6:7, :]
             power[pl.ds(half + k, 1), :] = tile[7:8, :]
+
+    @pl.loop(1, half // 2 - 1)
+    def _(at):
+        turn_last((2 * at, 2 * at + 1))
+
+    if half > 2:
+        turn_last((1, half - 2))
+    turn_last((0, half - 1))
 
     for side, lent, lender in ((0, has_next, half - 1), (1, has_last, 0)):
 

time: 32.5 us -> 31.2 us (0.960)
  Pallas kernels: 27.8 us -> 26.5 us
    pallas_call x1, Pallas kernels: 27.8 us -> 26.5 us  [per_device(): pl.pallas_call(functools.partial(turning_kernel, n, n_pairs, half, rows),...]
where the time goes in v9:
time: 31.2 us; the launch traced here: 31 us
  Pallas kernels  26.5 us (85%)
  local copies, waits for them, and re-layouts  1.93 us (6%)
  other arithmetic  1.89 us (6%)
  between operations  0.68 us (2%)
    pallas_call x1, Pallas kernels, per_device(): pl.pallas_call(functools.partial(turning_kernel, n, n_pairs, half, rows),...  26.5 us
    unnamed x6, local copies, waits for them, and re-layouts  1.93 us
    mul x1, other arithmetic, per_device(): weighted = loads * col_weights[None, :]  1.89 us

profile of v9, /device:TPU:0, one launch (start us, length us, event | category | flops | bytes accessed | tf_op | source)
XLA Modules:
  0.0 31.0 jit_solution(17763514293748215681)
XLA Ops:
  0.6 0.0 copy-start.1
  0.6 0.0 copy-start
  0.7 1.9 %broadcast_multiply_fusion.data = f32[256,2048]{1,0:T(8,128)S(1)} fusion(f32[256,2048]{1,0:T(8,128)} %param.4, f32[2048]{0:T(1024)} %param.5), kind=kLoop, calls=%fused_computation | loop fusion | flops 524288 | bytes 4202496 | tf_op jit(solution)/shard_map/mul | solution.py:405
  2.5 0.0 copy-done.1
  2.6 0.0 copy-done
  2.6 26.5 %shard_map.59 = (f32[256,2048]{1,0:T(8,128)S(1)}, f32[16,128]{1,0:T(8,128)S(1)}) custom-call(f32[256,2048]{1,0:T(8,128)S(1)} %broadcast_multiply_fusion.data, s32[2,2]{1,0:T(2,128)S(1)} %copy-done, s32[2,8]{1,0:T(2,128)S(1)} %copy-done.1), custom_call_target="tpu_custom_call" | custom-call | flops 31457280 | bytes 4194304 | tf_op jit(solution)/shard_map/pallas_call | solution.py:406
  29.1 1.3 %copy.8 = f32[256,2048]{1,0:T(8,128)} copy(f32[256,2048]{1,0:T(8,128)S(1)} %get-tuple-element.8) | data formatting | bytes 4194304
  30.4 0.6 %copy.9 = f32[2048]{0:T(1024)} copy(f32[2048]{0:T(1024)S(1)} %bitcast.1) | data formatting | bytes 16384
Async XLA Ops:
  0.6 1.9 %copy-start.1 = (s32[2,8]{1,0:T(2,128)S(1)}, s32[2,8]{1,0:T(2,128)}, u32[]{:S(2)}) copy-start(s32[2,8]{1,0:T(2,128)} %skips.1) | copy-start | bytes 196
  0.6 1.9 %copy-start = (s32[2,2]{1,0:T(2,128)S(1)}, s32[2,2]{1,0:T(2,128)}, u32[]{:S(2)}) copy-start(s32[2,2]{1,0:T(2,128)} %offsets.1) | copy-start | bytes 52

commit v10 on v9

--- a/solution.py
+++ b/solution.py
@@ -145,6 +145,14 @@
     later.end()
 
 
+def each(least, end):
+    def run(body):
+        for at in range(least, end):
+            body(at)
+
+    return run
+
+
 def column_block(array, block):
     return array.at[:, pl.ds(pl.multiple_of(block * BLOCK, BLOCK), BLOCK)]
 
@@ -164,7 +172,7 @@
 
     barrier = pltpu.get_barrier_semaphore()
 
-    @pl.loop(1, n)
+    @each(1, n)
     def _(by):
         pl.semaphore_signal(
             barrier, inc=1, device_id={"rows": lax.rem(me + by, n)}, device_id_type=MESH
@@ -173,7 +181,7 @@
     def greet_pairs(to):
         pl.semaphore_signal(barrier, inc=1, device_id={"pairs": to}, device_id_type=MESH)
 
-        @pl.loop(0, half)
+        @each(0, half)
         def _(at):
             pl.semaphore_signal(
                 barrier, inc=1,
@@ -189,7 +197,7 @@
         greet_pairs(position + 1)
 
     def give(step, k):
-        @pl.loop(0, copies)
+        @each(0, copies)
         def _(at):
             to = k * copies + at
 
@@ -214,7 +222,7 @@
         total = jnp.sum(arrived[step], axis=0)
         coefs[step, own] = turn(total, skips[step, own], shifts)
 
-        @pl.loop(1, half)
+        @each(1, half)
         def _(by):
             to = lax.rem(own + by, half) * copies + group
             pltpu.make_async_remote_copy(
@@ -241,7 +249,7 @@
             ).start()
 
     def lend_coefs(k, side, to):
-        @pl.loop(0, half)
+        @each(0, half)
         def _(at):
             pltpu.make_async_remote_copy(
                 src_ref=coefs.at[0, k],

time: 31.2 us -> 31 us (level)
  no operation moved by 1% of the time
where the time goes in v10:
time: 31 us; the launch traced here: 30.9 us
  Pallas kernels  26.4 us (85%)
  local copies, waits for them, and re-layouts  1.93 us (6%)
  other arithmetic  1.89 us (6%)
  between operations  0.68 us (2%)
    pallas_call x1, Pallas kernels, per_device(): pl.pallas_call(functools.partial(turning_kernel, n, n_pairs, half, rows),...  26.4 us
    unnamed x6, local copies, waits for them, and re-layouts  1.93 us
    mul x1, other arithmetic, per_device(): weighted = loads * col_weights[None, :]  1.89 us

profile of v10, /device:TPU:0, one launch (start us, length us, event | category | flops | bytes accessed | tf_op | source)
XLA Modules:
  0.0 30.9 jit_solution(10513262190853962635)
XLA Ops:
  0.6 0.0 copy-start.1
  0.6 0.0 copy-start
  0.7 1.9 %broadcast_multiply_fusion.data = f32[256,2048]{1,0:T(8,128)S(1)} fusion(f32[256,2048]{1,0:T(8,128)} %param.4, f32[2048]{0:T(1024)} %param.5), kind=kLoop, calls=%fused_computation | loop fusion | flops 524288 | bytes 4202496 | tf_op jit(solution)/shard_map/mul | solution.py:413
  2.5 0.0 copy-done.1
  2.6 0.0 copy-done
  2.6 26.4 %shard_map.59 = (f32[256,2048]{1,0:T(8,128)S(1)}, f32[16,128]{1,0:T(8,128)S(1)}) custom-call(f32[256,2048]{1,0:T(8,128)S(1)} %broadcast_multiply_fusion.data, s32[2,2]{1,0:T(2,128)S(1)} %copy-done, s32[2,8]{1,0:T(2,128)S(1)} %copy-done.1), custom_call_target="tpu_custom_call" | custom-call | flops 31457280 | bytes 4194304 | tf_op jit(solution)/shard_map/pallas_call | solution.py:414
  28.9 1.3 %copy.8 = f32[256,2048]{1,0:T(8,128)} copy(f32[256,2048]{1,0:T(8,128)S(1)} %get-tuple-element.8) | data formatting | bytes 4194304
  30.3 0.6 %copy.9 = f32[2048]{0:T(1024)} copy(f32[2048]{0:T(1024)S(1)} %bitcast.1) | data formatting | bytes 16384
Async XLA Ops:
  0.6 1.9 %copy-start.1 = (s32[2,8]{1,0:T(2,128)S(1)}, s32[2,8]{1,0:T(2,128)}, u32[]{:S(2)}) copy-start(s32[2,8]{1,0:T(2,128)} %skips.1) | copy-start | bytes 196
  0.6 1.9 %copy-start = (s32[2,2]{1,0:T(2,128)S(1)}, s32[2,2]{1,0:T(2,128)}, u32[]{:S(2)}) copy-start(s32[2,2]{1,0:T(2,128)} %offsets.1) | copy-start | bytes 52
